TPU v7x, 32 devices: a whole 2x2x4 slice. The times are simulated.
32 devices in a mesh: ctx: 8 (over z, core), tp: 4 (over y, x).
Axes of the slice: x: 2, y: 2, z: 4, core: 2. Of those that a mesh axis runs over, the one named last changes fastest.
Arguments:
- queries: bfloat16 [16384, 1024], P(('ctx', 'tp')), may hold values from -6 to 6, as said below
- keys: bfloat16 [16384, 512], P(('ctx', 'tp')), may hold values from -9 to 9, as said below
- values: bfloat16 [16384, 512], P(('ctx', 'tp')), may hold values from -5 to 5
- output_gradient: bfloat16 [16384, 1024], P(('ctx', 'tp')), may hold values from -5 to 5
Outputs:
- attn_out: bfloat16 [16384, 1024], P(('ctx', 'tp'))
- grad_q: bfloat16 [16384, 1024], P(('ctx', 'tp'))
- grad_k: bfloat16 [16384, 512], P(('ctx', 'tp'))
- grad_v: bfloat16 [16384, 512], P(('ctx', 'tp'))
Inputs may be any that keep to these rules, and one draw needn't show every extreme that they name: queries are real-valued. keys are real-valued.
All inputs are finite; a program needn't handle non-finite values.
Results may differ from a plain program's by a relative error of at most 0.023.
Values may be sent and summed in bfloat16 or wider, within the bound.
No kernel may reach another device: no remote copies, remote signals or barrier semaphores. Data moves between devices by JAX's collectives and lax.ppermute only.
A program may use at most 128 MiB of HBM per device.

v0:
```python
import functools
import math

import jax
import jax.numpy as jnp
from jax import lax
from jax.experimental import pallas as pl
from jax.experimental.pallas import tpu as pltpu
from jax.sharding import PartitionSpec as P

HEAD_SIZE = 128
QUERY_GROUP = 2
WINDOW_LENGTH = 1024
QSCALE = 168
ROWS = 256
TILES = WINDOW_LENGTH // ROWS + 1
AXES = ("ctx", "tp")
LOW = -1e30


def nt(a, b):
    return lax.dot_general(a, b, (((1,), (1,)), ((), ())), preferred_element_type=jnp.float32)


def tn(a, b):
    return lax.dot_general(a, b, (((0,), (0,)), ((), ())), preferred_element_type=jnp.float32)


def stacked(ref):
    return jnp.concatenate(
        [ref[:, g * HEAD_SIZE : (g + 1) * HEAD_SIZE] for g in range(QUERY_GROUP)], 0
    )


def attention_kernel(pieces, steps, absent_ref, q_ref, g_ref, *refs):
    key_refs = refs[: 2 * len(pieces)]
    n_alias = len(refs) - 4 - 2 * len(pieces) * 2
    outs = refs[2 * len(pieces) :]
    o_ref, dq_ref = outs[0], outs[1]
    grad_refs = outs[2 : 2 + 2 * len(pieces)]
    kx, vx, dkx, dvx, s_scr, p_scr = outs[2 + 2 * len(pieces) :]
    scale = QSCALE**-0.5
    c = scale * math.log2(math.e)
    r = pl.program_id(1)

    def at(ref, start, size):
        return ref.at[start : start + size] if len(ref.shape) == 2 else ref.at[0, start : start + size]

    @pl.when(r == 0)
    def _():
        row = 0
        for n, size in enumerate(pieces):
            kx[row : row + size] = key_refs[2 * n][...].reshape(size, HEAD_SIZE)
            vx[row : row + size] = key_refs[2 * n + 1][...].reshape(size, HEAD_SIZE)
            row += size
        dkx[...] = jnp.zeros_like(dkx)
        dvx[...] = jnp.zeros_like(dvx)

    absent = absent_ref[0]
    base = pl.multiple_of(r * ROWS, ROWS)
    qs = stacked(q_ref)
    gs = stacked(g_ref)
    width = QUERY_GROUP * ROWS
    key_at = lax.broadcasted_iota(jnp.int32, (ROWS, width), 0)
    query_at = lax.broadcasted_iota(jnp.int32, (ROWS, width), 1) % ROWS
    upto = key_at <= query_at

    def rows(ref, t):
        return ref[pl.ds(base + t * ROWS, ROWS), :]

    top = jnp.full((1, width), LOW, jnp.float32)
    for t in range(TILES):
        s = nt(rows(kx, t), qs)
        if t == 0:
            s = jnp.where(upto, LOW, s)
        if t == TILES - 1:
            s = jnp.where(upto, s, LOW)
        s_scr[t] = s
        best = jnp.max(s, axis=0, keepdims=True)
        if t < TILES - 1:
            best = jnp.where(base + t * ROWS >= absent, best, LOW)
        top = jnp.maximum(top, best)
    top = top * c
    total = jnp.zeros((1, width), jnp.float32)
    out = jnp.zeros((HEAD_SIZE, width), jnp.float32)
    for t in range(TILES):
        lift = top if t == TILES - 1 else jnp.where(base + t * ROWS >= absent, top, -LOW)
        p = jnp.exp2(s_scr[t] * c - lift)
        total += jnp.sum(p, axis=0, keepdims=True)
        p_low = p.astype(jnp.bfloat16)
        p_scr[t] = p_low
        out += tn(rows(vx, t), p_low)
    inverse = 1.0 / total
    out_low = (out * inverse).astype(jnp.bfloat16).astype(jnp.float32)
    delta = jnp.sum(gs.astype(jnp.float32).T * out_low, axis=0, keepdims=True)
    out_rows = out_low.T.astype(jnp.bfloat16)
    column = jnp.broadcast_to(inverse, (HEAD_SIZE, width)).T
    q_part = (qs.astype(jnp.float32) * (column * scale)).astype(jnp.bfloat16)
    g_part = (gs.astype(jnp.float32) * column).astype(jnp.bfloat16)
    dq = jnp.zeros((HEAD_SIZE, width), jnp.float32)
    for t in range(TILES):
        here = pl.ds(base + t * ROWS, ROWS)
        p_low = p_scr[t]
        dp = nt(rows(vx, t), gs)
        ds = (p_low.astype(jnp.float32) * (dp - delta)).astype(jnp.bfloat16)
        dvx[here, :] += jnp.dot(p_low, g_part, preferred_element_type=jnp.float32)
        dkx[here, :] += jnp.dot(ds, q_part, preferred_element_type=jnp.float32)
        dq += tn(rows(kx, t), ds)
    dq_rows = (dq * (inverse * scale)).T.astype(jnp.bfloat16)
    for g in range(QUERY_GROUP):
        o_ref[:, g * HEAD_SIZE : (g + 1) * HEAD_SIZE] = out_rows[g * ROWS : (g + 1) * ROWS]
        dq_ref[:, g * HEAD_SIZE : (g + 1) * HEAD_SIZE] = dq_rows[g * ROWS : (g + 1) * ROWS]

    @pl.when(r == steps - 1)
    def _():
        row = 0
        for n, size in enumerate(pieces):
            for ref, wide in ((grad_refs[2 * n], dkx), (grad_refs[2 * n + 1], dvx)):
                ref[...] = wide[row : row + size].reshape(ref.shape).astype(ref.dtype)
            row += size


def flat_rows(width):
    return lambda spec: spec


def attention(absent, queries, grads, keys, values, before, head, heads, earlier):
    tokens = queries.shape[0]
    steps = tokens // ROWS
    group = QUERY_GROUP * HEAD_SIZE
    pieces = tuple(b.shape[2] for b in before) + (tokens,)
    wide = pl.BlockSpec((ROWS, group), lambda h, r: (r, head + h))
    own = pl.BlockSpec((tokens, HEAD_SIZE), lambda h, r: (0, head + h))

    def part(n, size):
        return pl.BlockSpec((1, 1, size, HEAD_SIZE), lambda h, r: (h, n, 0, 0))

    in_specs = [pl.BlockSpec(memory_space=pltpu.SMEM), wide, wide]
    args = [absent, queries, grads]
    out_specs = [wide, wide]
    out_shape = [jax.ShapeDtypeStruct(queries.shape, jnp.bfloat16)] * 2
    for b in before:
        size = b.shape[2]
        in_specs += [part(0, size), part(1, size)]
        args += [b, b]
        for n in range(2):
            out_specs.append(pl.BlockSpec((1, size, HEAD_SIZE), lambda h, r: (h, 0, 0)))
            out_shape.append(jax.ShapeDtypeStruct((heads, size, HEAD_SIZE), jnp.bfloat16))
    in_specs += [own, own]
    args += [keys, values]
    for n in range(2):
        out_specs.append(pl.BlockSpec((1, tokens, HEAD_SIZE), lambda h, r: (h, 0, 0)))
        out_shape.append(jax.ShapeDtypeStruct((heads, tokens, HEAD_SIZE), jnp.float32))
    extent = sum(pieces)
    width = QUERY_GROUP * ROWS
    aliases = {}
    body = functools.partial(attention_kernel, pieces, steps)
    if earlier is not None:
        n_in = len(args)
        in_specs += [pl.BlockSpec(memory_space=pl.ANY)] * 2
        args += list(earlier)
        aliases = {n_in: 0, n_in + 1: 1}
        inner = body

        def body(*refs):
            inner(*refs[:n_in], *refs[n_in + 2 :])

    pairs = heads * tokens * QUERY_GROUP * TILES * ROWS
    return pl.pallas_call(
        body,
        grid=(heads, steps),
        in_specs=in_specs,
        out_specs=out_specs,
        out_shape=out_shape,
        scratch_shapes=[
            pltpu.VMEM((extent, HEAD_SIZE), jnp.bfloat16),
            pltpu.VMEM((extent, HEAD_SIZE), jnp.bfloat16),
            pltpu.VMEM((extent, HEAD_SIZE), jnp.float32),
            pltpu.VMEM((extent, HEAD_SIZE), jnp.float32),
            pltpu.VMEM((TILES, ROWS, width), jnp.float32),
            pltpu.VMEM((TILES, ROWS, width), jnp.bfloat16),
        ],
        input_output_aliases=aliases,
        compiler_params=pltpu.CompilerParams(
            dimension_semantics=("arbitrary", "arbitrary"), vmem_limit_bytes=40 * 2**20
        ),
        cost_estimate=pl.CostEstimate(
            flops=24 * HEAD_SIZE * pairs, bytes_accessed=8 * 2**20 * heads // 4, transcendentals=pairs
        ),
        name="attention",
    )(*args)


def head_parts(keys, values, head, heads):
    rows = keys.shape[0]
    span = slice(head * HEAD_SIZE, (head + heads) * HEAD_SIZE)
    both = jnp.stack([keys[:, span], values[:, span]], 0).reshape(2, rows, heads, HEAD_SIZE)
    return both.transpose(2, 0, 1, 3)


def side_by_side(parts):
    return parts.transpose(1, 0, 2).reshape(parts.shape[1], -1)


CHUNKS = 4


def by_tokens(queries, keys, values, output_gradient):
    count = lax.axis_size(AXES)
    me = lax.axis_index(AXES)
    odd = me % 2 == 1
    rows = queries.shape[0]
    ahead = [(i, i + 2) for i in range(count - 2)]
    back = [(i + 2, i) for i in range(count - 2)]
    swap = [(i, i ^ 1) for i in range(count)]
    absent = jnp.maximum(WINDOW_LENGTH - me * rows, 0).astype(jnp.int32).reshape(1)
    kv_heads = keys.shape[1] // HEAD_SIZE
    heads = kv_heads // CHUNKS
    outs = None
    key_grads, value_grads = [], []
    starts = [h * heads for h in range(CHUNKS)]
    mine = [head_parts(keys, values, h, heads) for h in starts]
    far = [lax.ppermute(x, AXES, ahead) for x in mine]
    near = [lax.ppermute(jnp.where(odd, f, x), AXES, swap) for x, f in zip(mine, far)]
    for n, h in enumerate(starts):
        o, dq, fk, fv, nk, nv, ok, ov = attention(
            absent, queries, output_gradient, keys, values, (far[n], near[n]), h, heads, outs
        )
        outs = (o, dq)
        near_back = [lax.ppermute(x, AXES, swap) for x in (nk, nv)]
        relay = [jnp.where(odd, x.astype(jnp.float32) + y.astype(jnp.float32), x.astype(jnp.float32)).astype(jnp.bfloat16) for x, y in zip((fk, fv), near_back)]
        far_back = [lax.ppermute(x, AXES, back) for x in relay]
        for own, x, y, grads in zip((ok, ov), near_back, far_back, (key_grads, value_grads)):
            total = own + y.astype(jnp.float32) + jnp.where(odd, 0.0, x.astype(jnp.float32))
            grads.append(side_by_side(total.astype(jnp.bfloat16)))
    return (*outs, jnp.concatenate(key_grads, 1), jnp.concatenate(value_grads, 1))


def by_heads(queries, keys, values, output_gradient):
    tp = lax.axis_size("tp")
    ctx = lax.axis_size("ctx")

    def gathered(x):
        return lax.all_to_all(x, "tp", split_axis=1, concat_axis=0, tiled=True)

    def returned(x):
        return lax.all_to_all(x, "tp", split_axis=0, concat_axis=1, tiled=True)

    queries, keys, values, grads = map(gathered, (queries, keys, values, output_gradient))
    rows = queries.shape[0]
    kv_heads = keys.shape[1] // HEAD_SIZE
    tail = head_parts(keys[rows - WINDOW_LENGTH :], values[rows - WINDOW_LENGTH :], 0, kv_heads)
    rim = lax.ppermute(tail, "ctx", [(i, i + 1) for i in range(ctx - 1)])
    first = lax.axis_index("ctx") == 0
    absent = jnp.where(first, WINDOW_LENGTH, 0).astype(jnp.int32).reshape(1)
    o, dq, fk, fv, ok, ov = attention(
        absent, queries, grads, keys, values, (rim,), 0, kv_heads, None
    )
    results = [o, dq]
    for own, rim_grad in ((ok, fk), (ov, fv)):
        back = lax.ppermute(rim_grad, "ctx", [(i + 1, i) for i in range(ctx - 1)])
        own = own.at[:, rows - WINDOW_LENGTH :].add(back.astype(jnp.float32))
        results.append(side_by_side(own.astype(jnp.bfloat16)))
    return tuple(map(returned, results))


def on_device(queries, keys, values, output_gradient):
    rows = queries.shape[0]
    if 2 * rows == WINDOW_LENGTH and lax.axis_size(AXES) % 2 == 0:
        return by_tokens(queries, keys, values, output_gradient)
    return by_heads(queries, keys, values, output_gradient)


def solution(mesh):
    spec = P(AXES, None)
    return jax.shard_map(
        on_device, mesh=mesh, in_specs=(spec,) * 4, out_specs=(spec,) * 4, check_vma=False
    )
```

profile of v0, /device:TPU:0, one launch (start us, length us, event | category | flops | bytes accessed | tf_op | source)
XLA Modules:
  0.0 97.3 jit_solution(1305226522679326818)
XLA Ops:
  2.1 4.9 %collective-permute-start = (bf16[1,2,512,128]{3,2,1,0:T(8,128)(2,1)S(1)}, bf16[1,2,512,128]{3,2,1,0:T(8,128)(2,1)S(1)}, u32[]{:S(2)}, u32[]{:S(2)}) collective-permute-start(bf16[1,2,512,128]{3,2,1,0:T(8,128)(2,1)S(1)} %maximum_bitcast_fusion), channel_id=1, source_target_pairs={{0,2},{1,3},{2,4},{3,5},{4,6},{5,7},{6,8},{7,9},{8,10},{9,11},{10,... | collective-permute-start | bytes 786440 | tf_op jit(solution)/shard_map/ppermute | solution.py:223
  7.0 1.9 %collective-permute-start.2 = (bf16[1,2,512,128]{3,2,1,0:T(8,128)(2,1)S(1)}, bf16[1,2,512,128]{3,2,1,0:T(8,128)(2,1)S(1)}, u32[]{:S(2)}, u32[]{:S(2)}) collective-permute-start(bf16[1,2,512,128]{3,2,1,0:T(8,128)(2,1)S(1)} %maximum_bitcast_fusion.1), channel_id=1, source_target_pairs={{0,2},{1,3},{2,4},{3,5},{4,6},{5,7},{6,8},{7,9},{8,10},{9,11},{10,... | collective-permute-start | bytes 786440 | tf_op jit(solution)/shard_map/ppermute | solution.py:223
  9.0 3.1 %collective-permute-start.6 = (bf16[1,2,512,128]{3,2,1,0:T(8,128)(2,1)S(1)}, bf16[1,2,512,128]{3,2,1,0:T(8,128)(2,1)S(1)}, u32[]{:S(2)}, u32[]{:S(2)}) collective-permute-start(bf16[1,2,512,128]{3,2,1,0:T(8,128)(2,1)S(1)} %maximum_bitcast_fusion.3), channel_id=1, source_target_pairs={{0,2},{1,3},{2,4},{3,5},{4,6},{5,7},{6,8},{7,9},{8,10},{9,11},{10,... | collective-permute-start | bytes 786440 | tf_op jit(solution)/shard_map/ppermute | solution.py:223
  12.1 3.7 %collective-permute-start.4 = (bf16[1,2,512,128]{3,2,1,0:T(8,128)(2,1)S(1)}, bf16[1,2,512,128]{3,2,1,0:T(8,128)(2,1)S(1)}, u32[]{:S(2)}, u32[]{:S(2)}) collective-permute-start(bf16[1,2,512,128]{3,2,1,0:T(8,128)(2,1)S(1)} %maximum_bitcast_fusion.2), channel_id=1, source_target_pairs={{0,2},{1,3},{2,4},{3,5},{4,6},{5,7},{6,8},{7,9},{8,10},{9,11},{10,... | collective-permute-start | bytes 786440 | tf_op jit(solution)/shard_map/ppermute | solution.py:223
  15.9 1.6 %collective-permute-start.1 = (bf16[1,2,512,128]{3,2,1,0:T(8,128)(2,1)S(1)}, bf16[1,2,512,128]{3,2,1,0:T(8,128)(2,1)S(1)}, u32[]{:S(2)}, u32[]{:S(2)}) collective-permute-start(bf16[1,2,512,128]{3,2,1,0:T(8,128)(2,1)S(1)} %broadcast_select_fusion.3), channel_id=1, source_target_pairs={{0,1},{1,0},{2,3},{3,2},{4,5},{5,4},{6,7},{7,6},{8,9},{9,8},{10,11... | collective-permute-start | bytes 786440 | tf_op jit(solution)/shard_map/ppermute | solution.py:224
  17.4 7.4 %collective-permute-done.6.refs_0_.refs_1_ = bf16[1,2,512,128]{3,2,1,0:T(8,128)(2,1)S(1)} collective-permute-done((bf16[1,2,512,128]{3,2,1,0:T(8,128)(2,1)S(1)}, bf16[1,2,512,128]{3,2,1,0:T(8,128)(2,1)S(1)}, u32[]{:S(2)}, u32[]{:S(2)}) %collective-permute-start.6) | collective-permute-done | bytes 262176 | tf_op jit(solution)/shard_map/ppermute | solution.py:223
  24.9 1.6 %collective-permute-start.7 = (bf16[1,2,512,128]{3,2,1,0:T(8,128)(2,1)S(1)}, bf16[1,2,512,128]{3,2,1,0:T(8,128)(2,1)S(1)}, u32[]{:S(2)}, u32[]{:S(2)}) collective-permute-start(bf16[1,2,512,128]{3,2,1,0:T(8,128)(2,1)S(1)} %broadcast_select_fusion), channel_id=1, source_target_pairs={{0,1},{1,0},{2,3},{3,2},{4,5},{5,4},{6,7},{7,6},{8,9},{9,8},{10,11... | collective-permute-start | bytes 786440 | tf_op jit(solution)/shard_map/ppermute | solution.py:224
  27.1 2.2 %collective-permute-done.4.refs_3_.refs_4_ = bf16[1,2,512,128]{3,2,1,0:T(8,128)(2,1)S(1)} collective-permute-done((bf16[1,2,512,128]{3,2,1,0:T(8,128)(2,1)S(1)}, bf16[1,2,512,128]{3,2,1,0:T(8,128)(2,1)S(1)}, u32[]{:S(2)}, u32[]{:S(2)}) %collective-permute-start.4) | collective-permute-done | bytes 262176 | tf_op jit(solution)/shard_map/ppermute | solution.py:223
  29.4 1.6 %collective-permute-start.5 = (bf16[1,2,512,128]{3,2,1,0:T(8,128)(2,1)S(1)}, bf16[1,2,512,128]{3,2,1,0:T(8,128)(2,1)S(1)}, u32[]{:S(2)}, u32[]{:S(2)}) collective-permute-start(bf16[1,2,512,128]{3,2,1,0:T(8,128)(2,1)S(1)} %broadcast_select_fusion.1), channel_id=1, source_target_pairs={{0,1},{1,0},{2,3},{3,2},{4,5},{5,4},{6,7},{7,6},{8,9},{9,8},{10,11... | collective-permute-start | bytes 786440 | tf_op jit(solution)/shard_map/ppermute | solution.py:224
  30.9 3.3 %collective-permute-done.7.refs_2_.refs_3_ = bf16[1,2,512,128]{3,2,1,0:T(8,128)(2,1)S(1)} collective-permute-done((bf16[1,2,512,128]{3,2,1,0:T(8,128)(2,1)S(1)}, bf16[1,2,512,128]{3,2,1,0:T(8,128)(2,1)S(1)}, u32[]{:S(2)}, u32[]{:S(2)}) %collective-permute-start.7) | collective-permute-done | bytes 262176 | tf_op jit(solution)/shard_map/ppermute | solution.py:224
  34.2 6.1 %attention.4 = (bf16[512,1024]{1,0:T(8,128)(2,1)}, bf16[512,1024]{1,0:T(8,128)(2,1)}, bf16[1,512,128]{2,1,0:T(8,128)(2,1)S(1)}, bf16[1,512,128]{2,1,0:T(8,128)(2...) custom-call(s32[1]{0:T(128)} %bitcast.absent_ref.refs_0_, ...), custom_call_target="tpu_custom_call" | custom-call | flops 4026531840 | bytes 2097152 | tf_op jit(solution)/shard_map/attention/pallas_call | solution.py:169
  40.4 1.5 %collective-permute-start.8 = (bf16[1,512,128]{2,1,0:T(8,128)(2,1)S(1)}, bf16[1,512,128]{2,1,0:T(8,128)(2,1)S(1)}, u32[]{:S(2)}, u32[]{:S(2)}) collective-permute-start(bf16[1,512,128]{2,1,0:T(8,128)(2,1)S(1)} %get-tuple-element.46), channel_id=1, source_target_pairs={{0,1},{1,0},{2,3},{3,2},{4,5},{5,4},{6,7},{7,6},{8,9},{9,8},{10,11... | collective-permute-start | bytes 393224 | tf_op jit(solution)/shard_map/ppermute | solution.py:230
  42.4 2.7 %collective-permute-done.5.refs_5_.refs_6_ = bf16[1,2,512,128]{3,2,1,0:T(8,128)(2,1)S(1)} collective-permute-done((bf16[1,2,512,128]{3,2,1,0:T(8,128)(2,1)S(1)}, bf16[1,2,512,128]{3,2,1,0:T(8,128)(2,1)S(1)}, u32[]{:S(2)}, u32[]{:S(2)}) %collective-permute-start.5) | collective-permute-done | bytes 262176 | tf_op jit(solution)/shard_map/ppermute | solution.py:224
  45.0 6.1 %attention.5 = (bf16[512,1024]{1,0:T(8,128)(2,1)}, bf16[512,1024]{1,0:T(8,128)(2,1)}, bf16[1,512,128]{2,1,0:T(8,128)(2,1)S(1)}, bf16[1,512,128]{2,1,0:T(8,128)(2...) custom-call(s32[1]{0:T(128)} %bitcast.absent_ref.refs_0_, ...), custom_call_target="tpu_custom_call", output_to_operand_aliasing={{0}: (9, {}), {1}: (10, {})} | custom-call | flops 4026531840 | bytes 2097152 | tf_op jit(solution)/shard_map/attention/pallas_call | solution.py:169
  51.1 1.5 %collective-permute-start.10 = (bf16[1,512,128]{2,1,0:T(8,128)(2,1)S(1)}, bf16[1,512,128]{2,1,0:T(8,128)(2,1)S(1)}, u32[]{:S(2)}, u32[]{:S(2)}) collective-permute-start(bf16[1,512,128]{2,1,0:T(8,128)(2,1)S(1)} %get-tuple-element.49), channel_id=1, source_target_pairs={{0,1},{1,0},{2,3},{3,2},{4,5},{5,4},{6,7},{7,6},{8,9},{9,8},{10,11... | collective-permute-start | bytes 393224 | tf_op jit(solution)/shard_map/ppermute | solution.py:230
  53.2 6.1 %attention.6 = (bf16[512,1024]{1,0:T(8,128)(2,1)}, bf16[512,1024]{1,0:T(8,128)(2,1)}, bf16[1,512,128]{2,1,0:T(8,128)(2,1)S(1)}, bf16[1,512,128]{2,1,0:T(8,128)(2...) custom-call(s32[1]{0:T(128)} %bitcast.absent_ref.refs_0_, ...), custom_call_target="tpu_custom_call", output_to_operand_aliasing={{0}: (9, {}), {1}: (10, {})} | custom-call | flops 4026531840 | bytes 2097152 | tf_op jit(solution)/shard_map/attention/pallas_call | solution.py:169
  59.3 1.5 %collective-permute-start.12 = (bf16[1,512,128]{2,1,0:T(8,128)(2,1)S(1)}, bf16[1,512,128]{2,1,0:T(8,128)(2,1)S(1)}, u32[]{:S(2)}, u32[]{:S(2)}) collective-permute-start(bf16[1,512,128]{2,1,0:T(8,128)(2,1)S(1)} %get-tuple-element.52), channel_id=1, source_target_pairs={{0,1},{1,0},{2,3},{3,2},{4,5},{5,4},{6,7},{7,6},{8,9},{9,8},{10,11... | collective-permute-start | bytes 393224 | tf_op jit(solution)/shard_map/ppermute | solution.py:230
  60.7 6.1 %attention.7 = (bf16[512,1024]{1,0:T(8,128)(2,1)}, bf16[512,1024]{1,0:T(8,128)(2,1)}, bf16[1,512,128]{2,1,0:T(8,128)(2,1)S(1)}, bf16[1,512,128]{2,1,0:T(8,128)(2...) custom-call(s32[1]{0:T(128)} %bitcast.absent_ref.refs_0_, ...), custom_call_target="tpu_custom_call", output_to_operand_aliasing={{0}: (9, {}), {1}: (10, {})} | custom-call | flops 4026531840 | bytes 2097152 | tf_op jit(solution)/shard_map/attention/pallas_call | solution.py:169
  67.4 1.5 %collective-permute-start.14 = (bf16[1,512,128]{2,1,0:T(8,128)(2,1)S(1)}, bf16[1,512,128]{2,1,0:T(8,128)(2,1)S(1)}, u32[]{:S(2)}, u32[]{:S(2)}) collective-permute-start(bf16[1,512,128]{2,1,0:T(8,128)(2,1)S(1)} %get-tuple-element.55), channel_id=1, source_target_pairs={{0,1},{1,0},{2,3},{3,2},{4,5},{5,4},{6,7},{7,6},{8,9},{9,8},{10,11... | collective-permute-start | bytes 393224 | tf_op jit(solution)/shard_map/ppermute | solution.py:230
  80.6 1.8 %collective-permute-done.11 = bf16[1,512,128]{2,1,0:T(8,128)(2,1)S(1)} collective-permute-done((bf16[1,512,128]{2,1,0:T(8,128)(2,1)S(1)}, bf16[1,512,128]{2,1,0:T(8,128)(2,1)S(1)}, u32[]{:S(2)}, u32[]{:S(2)}) %collective-permute-start.11) | collective-permute-done | bytes 131104 | tf_op jit(solution)/shard_map/ppermute | solution.py:232
  85.3 2.7 %collective-permute-done.13 = bf16[1,512,128]{2,1,0:T(8,128)(2,1)S(1)} collective-permute-done((bf16[1,512,128]{2,1,0:T(8,128)(2,1)S(1)}, bf16[1,512,128]{2,1,0:T(8,128)(2,1)S(1)}, u32[]{:S(2)}, u32[]{:S(2)}) %collective-permute-start.13) | collective-permute-done | bytes 131104 | tf_op jit(solution)/shard_map/ppermute | solution.py:232
  88.1 2.7 %collective-permute-done.21 = bf16[1,512,128]{2,1,0:T(8,128)(2,1)S(1)} collective-permute-done((bf16[1,512,128]{2,1,0:T(8,128)(2,1)S(1)}, bf16[1,512,128]{2,1,0:T(8,128)(2,1)S(1)}, u32[]{:S(2)}, u32[]{:S(2)}) %collective-permute-start.21) | collective-permute-done | bytes 131104 | tf_op jit(solution)/shard_map/ppermute | solution.py:232
  90.9 2.7 %collective-permute-done.15 = bf16[1,512,128]{2,1,0:T(8,128)(2,1)S(1)} collective-permute-done((bf16[1,512,128]{2,1,0:T(8,128)(2,1)S(1)}, bf16[1,512,128]{2,1,0:T(8,128)(2,1)S(1)}, u32[]{:S(2)}, u32[]{:S(2)}) %collective-permute-start.15) | collective-permute-done | bytes 131104 | tf_op jit(solution)/shard_map/ppermute | solution.py:232
  94.5 1.9 %collective-permute-done.23 = bf16[1,512,128]{2,1,0:T(8,128)(2,1)S(1)} collective-permute-done((bf16[1,512,128]{2,1,0:T(8,128)(2,1)S(1)}, bf16[1,512,128]{2,1,0:T(8,128)(2,1)S(1)}, u32[]{:S(2)}, u32[]{:S(2)}) %collective-permute-start.23) | collective-permute-done | bytes 131104 | tf_op jit(solution)/shard_map/ppermute | solution.py:232
  (63 shorter events, 20.2 us)
Async XLA Ops:
  2.1 13.8 %collective-permute-start = (bf16[1,2,512,128]{3,2,1,0:T(8,128)(2,1)S(1)}, bf16[1,2,512,128]{3,2,1,0:T(8,128)(2,1)S(1)}, u32[]{:S(2)}, u32[]{:S(2)}) collective-permute-start(bf16[1,2,512,128]{3,2,1,0:T(8,128)(2,1)S(1)} %maximum_bitcast_fusion), channel_id=1, source_target_pairs={{0,2},{1,3},{2,4},{3,5},{4,6},{5,7},{6,8},{7,9},{8,10},{9,11},{10,... | collective-permute-start | bytes 786440 | tf_op jit(solution)/shard_map/ppermute | solution.py:223
  7.0 19.5 %collective-permute-start.2 = (bf16[1,2,512,128]{3,2,1,0:T(8,128)(2,1)S(1)}, bf16[1,2,512,128]{3,2,1,0:T(8,128)(2,1)S(1)}, u32[]{:S(2)}, u32[]{:S(2)}) collective-permute-start(bf16[1,2,512,128]{3,2,1,0:T(8,128)(2,1)S(1)} %maximum_bitcast_fusion.1), channel_id=1, source_target_pairs={{0,2},{1,3},{2,4},{3,5},{4,6},{5,7},{6,8},{7,9},{8,10},{9,11},{10,... | collective-permute-start | bytes 786440 | tf_op jit(solution)/shard_map/ppermute | solution.py:223
  9.0 15.9 %collective-permute-start.6 = (bf16[1,2,512,128]{3,2,1,0:T(8,128)(2,1)S(1)}, bf16[1,2,512,128]{3,2,1,0:T(8,128)(2,1)S(1)}, u32[]{:S(2)}, u32[]{:S(2)}) collective-permute-start(bf16[1,2,512,128]{3,2,1,0:T(8,128)(2,1)S(1)} %maximum_bitcast_fusion.3), channel_id=1, source_target_pairs={{0,2},{1,3},{2,4},{3,5},{4,6},{5,7},{6,8},{7,9},{8,10},{9,11},{10,... | collective-permute-start | bytes 786440 | tf_op jit(solution)/shard_map/ppermute | solution.py:223
  12.1 17.3 %collective-permute-start.4 = (bf16[1,2,512,128]{3,2,1,0:T(8,128)(2,1)S(1)}, bf16[1,2,512,128]{3,2,1,0:T(8,128)(2,1)S(1)}, u32[]{:S(2)}, u32[]{:S(2)}) collective-permute-start(bf16[1,2,512,128]{3,2,1,0:T(8,128)(2,1)S(1)} %maximum_bitcast_fusion.2), channel_id=1, source_target_pairs={{0,2},{1,3},{2,4},{3,5},{4,6},{5,7},{6,8},{7,9},{8,10},{9,11},{10,... | collective-permute-start | bytes 786440 | tf_op jit(solution)/shard_map/ppermute | solution.py:223
  15.9 43.4 %collective-permute-start.1 = (bf16[1,2,512,128]{3,2,1,0:T(8,128)(2,1)S(1)}, bf16[1,2,512,128]{3,2,1,0:T(8,128)(2,1)S(1)}, u32[]{:S(2)}, u32[]{:S(2)}) collective-permute-start(bf16[1,2,512,128]{3,2,1,0:T(8,128)(2,1)S(1)} %broadcast_select_fusion.3), channel_id=1, source_target_pairs={{0,1},{1,0},{2,3},{3,2},{4,5},{5,4},{6,7},{7,6},{8,9},{9,8},{10,11... | collective-permute-start | bytes 786440 | tf_op jit(solution)/shard_map/ppermute | solution.py:224
  24.9 9.3 %collective-permute-start.7 = (bf16[1,2,512,128]{3,2,1,0:T(8,128)(2,1)S(1)}, bf16[1,2,512,128]{3,2,1,0:T(8,128)(2,1)S(1)}, u32[]{:S(2)}, u32[]{:S(2)}) collective-permute-start(bf16[1,2,512,128]{3,2,1,0:T(8,128)(2,1)S(1)} %broadcast_select_fusion), channel_id=1, source_target_pairs={{0,1},{1,0},{2,3},{3,2},{4,5},{5,4},{6,7},{7,6},{8,9},{9,8},{10,11... | collective-permute-start | bytes 786440 | tf_op jit(solution)/shard_map/ppermute | solution.py:224
  26.5 26.1 %collective-permute-start.3 = (bf16[1,2,512,128]{3,2,1,0:T(8,128)(2,1)S(1)}, bf16[1,2,512,128]{3,2,1,0:T(8,128)(2,1)S(1)}, u32[]{:S(2)}, u32[]{:S(2)}) collective-permute-start(bf16[1,2,512,128]{3,2,1,0:T(8,128)(2,1)S(1)} %broadcast_select_fusion.2), channel_id=1, source_target_pairs={{0,1},{1,0},{2,3},{3,2},{4,5},{5,4},{6,7},{7,6},{8,9},{9,8},{10,11... | collective-permute-start | bytes 786440 | tf_op jit(solution)/shard_map/ppermute | solution.py:224
  29.4 15.7 %collective-permute-start.5 = (bf16[1,2,512,128]{3,2,1,0:T(8,128)(2,1)S(1)}, bf16[1,2,512,128]{3,2,1,0:T(8,128)(2,1)S(1)}, u32[]{:S(2)}, u32[]{:S(2)}) collective-permute-start(bf16[1,2,512,128]{3,2,1,0:T(8,128)(2,1)S(1)} %broadcast_select_fusion.1), channel_id=1, source_target_pairs={{0,1},{1,0},{2,3},{3,2},{4,5},{5,4},{6,7},{7,6},{8,9},{9,8},{10,11... | collective-permute-start | bytes 786440 | tf_op jit(solution)/shard_map/ppermute | solution.py:224
  40.4 26.5 %collective-permute-start.8 = (bf16[1,512,128]{2,1,0:T(8,128)(2,1)S(1)}, bf16[1,512,128]{2,1,0:T(8,128)(2,1)S(1)}, u32[]{:S(2)}, u32[]{:S(2)}) collective-permute-start(bf16[1,512,128]{2,1,0:T(8,128)(2,1)S(1)} %get-tuple-element.46), channel_id=1, source_target_pairs={{0,1},{1,0},{2,3},{3,2},{4,5},{5,4},{6,7},{7,6},{8,9},{9,8},{10,11... | collective-permute-start | bytes 393224 | tf_op jit(solution)/shard_map/ppermute | solution.py:230
  41.8 25.6 %collective-permute-start.16 = (bf16[1,512,128]{2,1,0:T(8,128)(2,1)S(1)}, bf16[1,512,128]{2,1,0:T(8,128)(2,1)S(1)}, u32[]{:S(2)}, u32[]{:S(2)}) collective-permute-start(bf16[1,512,128]{2,1,0:T(8,128)(2,1)S(1)} %get-tuple-element.58), channel_id=1, source_target_pairs={{0,1},{1,0},{2,3},{3,2},{4,5},{5,4},{6,7},{7,6},{8,9},{9,8},{10,11... | collective-permute-start | bytes 393224 | tf_op jit(solution)/shard_map/ppermute | solution.py:230
  51.1 17.9 %collective-permute-start.10 = (bf16[1,512,128]{2,1,0:T(8,128)(2,1)S(1)}, bf16[1,512,128]{2,1,0:T(8,128)(2,1)S(1)}, u32[]{:S(2)}, u32[]{:S(2)}) collective-permute-start(bf16[1,512,128]{2,1,0:T(8,128)(2,1)S(1)} %get-tuple-element.49), channel_id=1, source_target_pairs={{0,1},{1,0},{2,3},{3,2},{4,5},{5,4},{6,7},{7,6},{8,9},{9,8},{10,11... | collective-permute-start | bytes 393224 | tf_op jit(solution)/shard_map/ppermute | solution.py:230
  52.6 17.1 %collective-permute-start.18 = (bf16[1,512,128]{2,1,0:T(8,128)(2,1)S(1)}, bf16[1,512,128]{2,1,0:T(8,128)(2,1)S(1)}, u32[]{:S(2)}, u32[]{:S(2)}) collective-permute-start(bf16[1,512,128]{2,1,0:T(8,128)(2,1)S(1)} %get-tuple-element.61), channel_id=1, source_target_pairs={{0,1},{1,0},{2,3},{3,2},{4,5},{5,4},{6,7},{7,6},{8,9},{9,8},{10,11... | collective-permute-start | bytes 393224 | tf_op jit(solution)/shard_map/ppermute | solution.py:230
  59.3 11.8 %collective-permute-start.12 = (bf16[1,512,128]{2,1,0:T(8,128)(2,1)S(1)}, bf16[1,512,128]{2,1,0:T(8,128)(2,1)S(1)}, u32[]{:S(2)}, u32[]{:S(2)}) collective-permute-start(bf16[1,512,128]{2,1,0:T(8,128)(2,1)S(1)} %get-tuple-element.52), channel_id=1, source_target_pairs={{0,1},{1,0},{2,3},{3,2},{4,5},{5,4},{6,7},{7,6},{8,9},{9,8},{10,11... | collective-permute-start | bytes 393224 | tf_op jit(solution)/shard_map/ppermute | solution.py:230
  66.8 5.6 %collective-permute-start.20 = (bf16[1,512,128]{2,1,0:T(8,128)(2,1)S(1)}, bf16[1,512,128]{2,1,0:T(8,128)(2,1)S(1)}, u32[]{:S(2)}, u32[]{:S(2)}) collective-permute-start(bf16[1,512,128]{2,1,0:T(8,128)(2,1)S(1)} %get-tuple-element.64), channel_id=1, source_target_pairs={{0,1},{1,0},{2,3},{3,2},{4,5},{5,4},{6,7},{7,6},{8,9},{9,8},{10,11... | collective-permute-start | bytes 393224 | tf_op jit(solution)/shard_map/ppermute | solution.py:230
  67.4 6.4 %collective-permute-start.14 = (bf16[1,512,128]{2,1,0:T(8,128)(2,1)S(1)}, bf16[1,512,128]{2,1,0:T(8,128)(2,1)S(1)}, u32[]{:S(2)}, u32[]{:S(2)}) collective-permute-start(bf16[1,512,128]{2,1,0:T(8,128)(2,1)S(1)} %get-tuple-element.55), channel_id=1, source_target_pairs={{0,1},{1,0},{2,3},{3,2},{4,5},{5,4},{6,7},{7,6},{8,9},{9,8},{10,11... | collective-permute-start | bytes 393224 | tf_op jit(solution)/shard_map/ppermute | solution.py:230
  69.0 6.1 %collective-permute-start.22 = (bf16[1,512,128]{2,1,0:T(8,128)(2,1)S(1)}, bf16[1,512,128]{2,1,0:T(8,128)(2,1)S(1)}, u32[]{:S(2)}, u32[]{:S(2)}) collective-permute-start(bf16[1,512,128]{2,1,0:T(8,128)(2,1)S(1)} %get-tuple-element.67), channel_id=1, source_target_pairs={{0,1},{1,0},{2,3},{3,2},{4,5},{5,4},{6,7},{7,6},{8,9},{9,8},{10,11... | collective-permute-start | bytes 393224 | tf_op jit(solution)/shard_map/ppermute | solution.py:230
  69.7 7.3 %collective-permute-start.9 = (bf16[1,512,128]{2,1,0:T(8,128)(2,1)S(1)}, bf16[1,512,128]{2,1,0:T(8,128)(2,1)S(1)}, u32[]{:S(2)}, u32[]{:S(2)}) collective-permute-start(bf16[1,512,128]{2,1,0:T(8,128)(2,1)S(1)} %fusion.16), channel_id=1, source_target_pairs={{2,0},{3,1},{4,2},{5,3},{6,4},{7,5},{8,6},{9,7},{10,8},{11,9},{12,... | collective-permute-start | bytes 393224 | tf_op jit(solution)/shard_map/ppermute | solution.py:232
  71.1 8.2 %collective-permute-start.17 = (bf16[1,512,128]{2,1,0:T(8,128)(2,1)S(1)}, bf16[1,512,128]{2,1,0:T(8,128)(2,1)S(1)}, u32[]{:S(2)}, u32[]{:S(2)}) collective-permute-start(bf16[1,512,128]{2,1,0:T(8,128)(2,1)S(1)} %fusion.20), channel_id=1, source_target_pairs={{2,0},{3,1},{4,2},{5,3},{6,4},{7,5},{8,6},{9,7},{10,8},{11,9},{12,... | collective-permute-start | bytes 393224 | tf_op jit(solution)/shard_map/ppermute | solution.py:232
  72.4 10.0 %collective-permute-start.11 = (bf16[1,512,128]{2,1,0:T(8,128)(2,1)S(1)}, bf16[1,512,128]{2,1,0:T(8,128)(2,1)S(1)}, u32[]{:S(2)}, u32[]{:S(2)}) collective-permute-start(bf16[1,512,128]{2,1,0:T(8,128)(2,1)S(1)} %fusion.17), channel_id=1, source_target_pairs={{2,0},{3,1},{4,2},{5,3},{6,4},{7,5},{8,6},{9,7},{10,8},{11,9},{12,... | collective-permute-start | bytes 393224 | tf_op jit(solution)/shard_map/ppermute | solution.py:232
  73.8 11.4 %collective-permute-start.19 = (bf16[1,512,128]{2,1,0:T(8,128)(2,1)S(1)}, bf16[1,512,128]{2,1,0:T(8,128)(2,1)S(1)}, u32[]{:S(2)}, u32[]{:S(2)}) collective-permute-start(bf16[1,512,128]{2,1,0:T(8,128)(2,1)S(1)} %fusion.21), channel_id=1, source_target_pairs={{2,0},{3,1},{4,2},{5,3},{6,4},{7,5},{8,6},{9,7},{10,8},{11,9},{12,... | collective-permute-start | bytes 393224 | tf_op jit(solution)/shard_map/ppermute | solution.py:232
  75.2 12.8 %collective-permute-start.13 = (bf16[1,512,128]{2,1,0:T(8,128)(2,1)S(1)}, bf16[1,512,128]{2,1,0:T(8,128)(2,1)S(1)}, u32[]{:S(2)}, u32[]{:S(2)}) collective-permute-start(bf16[1,512,128]{2,1,0:T(8,128)(2,1)S(1)} %fusion.18), channel_id=1, source_target_pairs={{2,0},{3,1},{4,2},{5,3},{6,4},{7,5},{8,6},{9,7},{10,8},{11,9},{12,... | collective-permute-start | bytes 393224 | tf_op jit(solution)/shard_map/ppermute | solution.py:232
  77.0 13.8 %collective-permute-start.21 = (bf16[1,512,128]{2,1,0:T(8,128)(2,1)S(1)}, bf16[1,512,128]{2,1,0:T(8,128)(2,1)S(1)}, u32[]{:S(2)}, u32[]{:S(2)}) collective-permute-start(bf16[1,512,128]{2,1,0:T(8,128)(2,1)S(1)} %fusion.22), channel_id=1, source_target_pairs={{2,0},{3,1},{4,2},{5,3},{6,4},{7,5},{8,6},{9,7},{10,8},{11,9},{12,... | collective-permute-start | bytes 393224 | tf_op jit(solution)/shard_map/ppermute | solution.py:232
  79.3 14.4 %collective-permute-start.15 = (bf16[1,512,128]{2,1,0:T(8,128)(2,1)S(1)}, bf16[1,512,128]{2,1,0:T(8,128)(2,1)S(1)}, u32[]{:S(2)}, u32[]{:S(2)}) collective-permute-start(bf16[1,512,128]{2,1,0:T(8,128)(2,1)S(1)} %fusion.19), channel_id=1, source_target_pairs={{2,0},{3,1},{4,2},{5,3},{6,4},{7,5},{8,6},{9,7},{10,8},{11,9},{12,... | collective-permute-start | bytes 393224 | tf_op jit(solution)/shard_map/ppermute | solution.py:232
  82.4 14.0 %collective-permute-start.23 = (bf16[1,512,128]{2,1,0:T(8,128)(2,1)S(1)}, bf16[1,512,128]{2,1,0:T(8,128)(2,1)S(1)}, u32[]{:S(2)}, u32[]{:S(2)}) collective-permute-start(bf16[1,512,128]{2,1,0:T(8,128)(2,1)S(1)} %fusion.23), channel_id=1, source_target_pairs={{2,0},{3,1},{4,2},{5,3},{6,4},{7,5},{8,6},{9,7},{10,8},{11,9},{12,... | collective-permute-start | bytes 393224 | tf_op jit(solution)/shard_map/ppermute | solution.py:232
  (4 other events, 52.2 us)
where the time goes:
time: 98.5 us; the launch traced here: 97.3 us
  starting transfers between devices  37.4 us (38%)
  waiting for transfers between devices  30.4 us (31%)
  Pallas kernels  24.4 us (25%)
  other arithmetic  2.79 us (3%)
  local copies, waits for them, and re-layouts  1.41 us (1%)
  between operations  1 us (1%)
    pallas_call x4, Pallas kernels, attention(): pl.pallas_call(body, grid=(heads, steps), in_specs=in_specs, out_specs=ou...  24.4 us
    ppermute x8, waiting for transfers between devices, by_tokens(): far_back = [lax.ppermute(x, AXES, back) for x in relay]  14.8 us
    ppermute x4, starting transfers between devices, by_tokens(): far = [lax.ppermute(x, AXES, ahead) for x in mine]  13.6 us
    ppermute x8, starting transfers between devices, by_tokens(): far_back = [lax.ppermute(x, AXES, back) for x in relay]  10.3 us
    ppermute x4, waiting for transfers between devices, by_tokens(): far = [lax.ppermute(x, AXES, ahead) for x in mine]  9.64 us
    ppermute x8, starting transfers between devices, by_tokens(): near_back = [lax.ppermute(x, AXES, swap) for x in (nk, nv)]  8.24 us
    ppermute x4, waiting for transfers between devices, by_tokens(): lax.ppermute(jnp.where(odd, f, x), AXES, swap)  5.94 us
    ppermute x4, starting transfers between devices, by_tokens(): lax.ppermute(jnp.where(odd, f, x), AXES, swap)  5.27 us
  transfers between devices with their start and end apart: 24, of which 12 were waited for; matrix products, arithmetic and copies ran while one was open for 2% of the time, Pallas kernels for 25%

commit v1 on v0

v1 whole, which is shorter than its diff:
```python
import functools
import math

import jax
import jax.numpy as jnp
from jax import lax
from jax.experimental import pallas as pl
from jax.experimental.pallas import tpu as pltpu
from jax.sharding import PartitionSpec as P

HEAD_SIZE = 128
QUERY_GROUP = 2
WINDOW_LENGTH = 1024
QSCALE = 168
BLOCK = 512
ROWS = 256
TILES = WINDOW_LENGTH // ROWS + 1
AXES = ("ctx", "tp")
LOW = -1e30


def nt(a, b):
    return lax.dot_general(a, b, (((1,), (1,)), ((), ())), preferred_element_type=jnp.float32)


def tn(a, b):
    return lax.dot_general(a, b, (((0,), (0,)), ((), ())), preferred_element_type=jnp.float32)


def attention_kernel(tokens, absent_ref, q_ref, g_ref, *refs):
    pieces = WINDOW_LENGTH // tokens + 1
    o_ref, dq_ref = refs[2 * pieces], refs[2 * pieces + 1]
    grad_refs = refs[2 * pieces + 2 : 3 * pieces + 2]
    s_scr, p_scr, d_scr, kt_scr, vt_scr, dkt_scr, dvt_scr = refs[3 * pieces + 2 :]
    scale = QSCALE**-0.5
    c = scale * math.log2(math.e)
    steps = tokens // ROWS
    width = QUERY_GROUP * ROWS
    span = TILES * ROWS
    absent = absent_ref[0]
    key_at = lax.broadcasted_iota(jnp.int32, (ROWS, ROWS), 0)
    query_at = lax.broadcasted_iota(jnp.int32, (ROWS, ROWS), 1)
    upto = key_at <= query_at

    def piece(which, n):
        ref = refs[2 * n + which]
        return ref[...].reshape(ref.shape[-2:])

    def tile(which, e):
        ref = refs[2 * (e // steps) + which]
        start = e % steps * ROWS
        if len(ref.shape) == 2:
            return ref[start : start + ROWS, :]
        return ref[0, 0, start : start + ROWS, :]

    def stacked(ref, r):
        return jnp.concatenate(
            [ref[r * ROWS : (r + 1) * ROWS, g * HEAD_SIZE : (g + 1) * HEAD_SIZE] for g in range(QUERY_GROUP)], 0
        )

    def unstacked(ref, r, x):
        for g in range(QUERY_GROUP):
            ref[r * ROWS : (r + 1) * ROWS, g * HEAD_SIZE : (g + 1) * HEAD_SIZE] = x[g * ROWS : (g + 1) * ROWS]

    def eights(x, op):
        return op(x.reshape(ROWS // 8, 8, ROWS), axis=0)

    for n in range(pieces):
        kt_scr[:, n * tokens : (n + 1) * tokens] = piece(0, n).T
        vt_scr[:, n * tokens : (n + 1) * tokens] = piece(1, n).T

    groups = range(QUERY_GROUP)

    def part(r):
        q_t, g_t = stacked(q_ref, r).T, stacked(g_ref, r).T
        cols = [slice(g * ROWS, (g + 1) * ROWS) for g in groups]
        tops = [jnp.full((8, ROWS), LOW, jnp.float32) for g in groups]
        for t in range(TILES):
            for g in groups:
                s = jnp.dot(tile(0, r + t), q_t[:, cols[g]], preferred_element_type=jnp.float32)
                if t == 0:
                    s = jnp.where(upto, LOW, s)
                if t == TILES - 1:
                    s = jnp.where(upto, s, LOW)
                s_scr[r, g, t] = s
                best = eights(s, jnp.max)
                if t < TILES - 1:
                    best = jnp.where((r + t) * ROWS >= absent, best, LOW)
                tops[g] = jnp.maximum(tops[g], best)
            yield
        tops = [jnp.max(x, axis=0, keepdims=True) * c for x in tops]
        totals = [jnp.zeros((8, ROWS), jnp.float32) for g in groups]
        for t in range(TILES):
            for g in groups:
                lift = tops[g] if t == TILES - 1 else jnp.where((r + t) * ROWS >= absent, tops[g], -LOW)
                p = jnp.exp2(s_scr[r, g, t] * c - lift)
                totals[g] += eights(p, jnp.sum)
                p_scr[r, t * ROWS : (t + 1) * ROWS, cols[g]] = p.astype(jnp.bfloat16)
            yield
        inverse = 1.0 / jnp.concatenate([jnp.sum(x, axis=0, keepdims=True) for x in totals], 1)
        out = jnp.dot(vt_scr[:, r * ROWS : r * ROWS + span], p_scr[r], preferred_element_type=jnp.float32)
        out_low = (out * inverse).astype(jnp.bfloat16)
        delta = jnp.sum(g_t.astype(jnp.float32) * out_low.astype(jnp.float32), axis=0, keepdims=True)
        unstacked(o_ref, r, out_low.T)
        q_part = (q_t.astype(jnp.float32) * (inverse * scale)).astype(jnp.bfloat16)
        g_part = (g_t.astype(jnp.float32) * inverse).astype(jnp.bfloat16)
        for t in range(TILES):
            for g in groups:
                dp = jnp.dot(tile(1, r + t), g_t[:, cols[g]], preferred_element_type=jnp.float32)
                here = slice(t * ROWS, (t + 1) * ROWS)
                p = p_scr[r, here, cols[g]].astype(jnp.float32)
                d_scr[r, here, cols[g]] = (p * (dp - delta[:, cols[g]])).astype(jnp.bfloat16)
            add(dvt_scr, nt(g_part, p_scr[r, here, :]), r, t)
            yield
        dq = jnp.dot(kt_scr[:, r * ROWS : r * ROWS + span], d_scr[r], preferred_element_type=jnp.float32)
        unstacked(dq_ref, r, (dq * (inverse * scale)).astype(jnp.bfloat16).T)
        for t in range(TILES):
            add(dkt_scr, nt(q_part, d_scr[r, t * ROWS : (t + 1) * ROWS, :]), r, t)
        yield

    def add(scr, x, r, t):
        here = slice((r + t) * ROWS, (r + t + 1) * ROWS)
        scr[:, here] = x if r == 0 or t == TILES - 1 else scr[:, here] + x

    running = [part(r) for r in range(steps)]
    for r in ORDER(steps):
        next(running[r], None)
    for n in range(pieces):
        for k, scr in enumerate((dkt_scr, dvt_scr)):
            grad_refs[n][0, k] = scr[:, n * tokens : (n + 1) * tokens].T.astype(grad_refs[n].dtype)


def in_turn(steps):
    return [r for r in range(steps) for _ in range(3 * TILES + 1)]


def staggered(steps):
    turns = []
    for stage in range(steps + 3):
        for _ in range(TILES + (stage >= 3)):
            turns += [r for r in range(steps) if 0 <= stage - r < 4]
    return turns


ORDER = staggered


def attention(absent, queries, grads, keys, values, before, head, heads, earlier):
    tokens = queries.shape[0]
    group = QUERY_GROUP * HEAD_SIZE
    wide = pl.BlockSpec((tokens, group), lambda h: (0, head + h))
    own = pl.BlockSpec((tokens, HEAD_SIZE), lambda h: (0, head + h))

    def part(n):
        return pl.BlockSpec((1, 1, tokens, HEAD_SIZE), lambda h: (h, n, 0, 0))

    in_specs = [pl.BlockSpec(memory_space=pltpu.SMEM), wide, wide]
    args = [absent, queries, grads]
    out_specs = [wide, wide]
    out_shape = [jax.ShapeDtypeStruct(queries.shape, jnp.bfloat16)] * 2
    for b in before:
        in_specs += [part(0), part(1)]
        args += [b, b]
    in_specs += [own, own]
    args += [keys, values]
    for kind in [jnp.bfloat16] * len(before) + [jnp.float32]:
        out_specs.append(pl.BlockSpec((1, 2, tokens, HEAD_SIZE), lambda h: (h, 0, 0, 0)))
        out_shape.append(jax.ShapeDtypeStruct((heads, 2, tokens, HEAD_SIZE), kind))
    width = QUERY_GROUP * ROWS
    extent = WINDOW_LENGTH + tokens
    steps = tokens // ROWS
    aliases = {}
    body = functools.partial(attention_kernel, tokens)
    if earlier is not None:
        n_in = len(args)
        in_specs += [pl.BlockSpec(memory_space=pl.ANY)] * 2
        args += list(earlier)
        aliases = {n_in: 0, n_in + 1: 1}
        inner = body

        def body(*refs):
            inner(*refs[:n_in], *refs[n_in + 2 :])

    pairs = heads * tokens * QUERY_GROUP * TILES * ROWS
    return pl.pallas_call(
        body,
        grid=(heads,),
        in_specs=in_specs,
        out_specs=out_specs,
        out_shape=out_shape,
        scratch_shapes=[
            pltpu.VMEM((steps, QUERY_GROUP, TILES, ROWS, ROWS), jnp.float32),
            pltpu.VMEM((steps, TILES * ROWS, width), jnp.bfloat16),
            pltpu.VMEM((steps, TILES * ROWS, width), jnp.bfloat16),
            pltpu.VMEM((HEAD_SIZE, extent), jnp.bfloat16),
            pltpu.VMEM((HEAD_SIZE, extent), jnp.bfloat16),
            pltpu.VMEM((HEAD_SIZE, extent), jnp.float32),
            pltpu.VMEM((HEAD_SIZE, extent), jnp.float32),
        ],
        input_output_aliases=aliases,
        compiler_params=pltpu.CompilerParams(
            dimension_semantics=("arbitrary",), vmem_limit_bytes=26 * 2**20
        ),
        cost_estimate=pl.CostEstimate(
            flops=12 * HEAD_SIZE * pairs, bytes_accessed=2 * 2**20 * heads, transcendentals=0
        ),
        name="attention",
    )(*args)


def head_parts(keys, values, head, heads):
    rows = keys.shape[0]
    span = slice(head * HEAD_SIZE, (head + heads) * HEAD_SIZE)
    both = jnp.stack([keys[:, span], values[:, span]], 0).reshape(2, rows, heads, HEAD_SIZE)
    return both.transpose(2, 0, 1, 3)


def side_by_side(parts):
    return parts.transpose(1, 0, 2).reshape(parts.shape[1], -1)


def after(x, *others):
    return lax.optimization_barrier((x, *others))[0] if others else x


def wide(x):
    return x.astype(jnp.float32)


CHUNKS = 4


def by_tokens(queries, keys, values, output_gradient):
    count = lax.axis_size(AXES)
    me = lax.axis_index(AXES)
    odd = me % 2 == 1
    rows = queries.shape[0]
    ahead = [(i, (i + 2) % count) for i in range(count)]
    back = [((i + 2) % count, i) for i in range(count)]
    swap = [(i, i ^ 1) for i in range(count)]
    absent = jnp.maximum(WINDOW_LENGTH - me * rows, 0).astype(jnp.int32).reshape(1)
    kv_heads = keys.shape[1] // HEAD_SIZE
    heads = kv_heads // CHUNKS
    far, send, near, relay, near_back, far_back, own = ({} for _ in range(7))
    mine = [head_parts(keys, values, n * heads, heads) for n in range(CHUNKS)]

    held = {n: () for n in range(CHUNKS)}

    def fetch_far(n):
        block = after(mine[n], *held[n])
        far[n] = lax.ppermute(block, AXES, ahead)

    def fetch_near(n):
        send[n] = jnp.where(odd, far[n], mine[n])
        near[n] = lax.ppermute(send[n], AXES, swap)

    def give_near(n):
        near_back[n] = lax.ppermute(to_near[n], AXES, swap)

    def give_far(n):
        relay[n] = jnp.where(odd, wide(to_far[n]) + wide(near_back[n]), wide(to_far[n])).astype(jnp.bfloat16)
        far_back[n] = lax.ppermute(relay[n], AXES, back)

    outs = None
    to_far, to_near = {}, {}

    def compute(n, *waits):
        nonlocal outs
        o, dq, to_far[n], to_near[n], own[n] = attention(
            after(absent, *waits), queries, output_gradient, keys, values, (far[n], near[n]), n * heads, heads, outs
        )
        outs = (o, dq)

    fetch_far(0)
    fetch_far(1)
    fetch_near(0)
    held[2] = (send[0],)
    fetch_far(2)
    fetch_near(1)
    held[3] = (far[1],)
    fetch_far(3)
    compute(0, send[1])
    give_near(0)
    far[2] = after(far[2], to_far[0])
    fetch_near(2)
    compute(1, send[2])
    give_near(1)
    far[3] = after(far[3], to_far[1])
    fetch_near(3)
    compute(2, send[3])
    give_near(2)
    near_back[0] = after(near_back[0], to_far[2])
    give_far(0)
    compute(3, relay[0])
    give_near(3)
    near_back[1] = after(near_back[1], to_far[3])
    give_far(1)
    give_far(2)
    give_far(3)
    key_grads, value_grads = [], []
    for n in range(CHUNKS):
        total = own[n] + wide(far_back[n]) + jnp.where(odd, 0.0, wide(near_back[n]))
        total = total.astype(jnp.bfloat16)
        for k, parts in enumerate((key_grads, value_grads)):
            parts += [total[h, k] for h in range(heads)]
    return (*outs, jnp.concatenate(key_grads, 1), jnp.concatenate(value_grads, 1))


def by_heads(queries, keys, values, output_gradient):
    tp = lax.axis_size("tp")
    ctx = lax.axis_size("ctx")

    def gathered(x):
        return lax.all_to_all(x, "tp", split_axis=1, concat_axis=0, tiled=True)

    def returned(x):
        return lax.all_to_all(x, "tp", split_axis=0, concat_axis=1, tiled=True)

    queries, keys, values, grads = map(gathered, (queries, keys, values, output_gradient))
    rows = queries.shape[0]
    kv_heads = keys.shape[1] // HEAD_SIZE
    tail = head_parts(keys[rows - WINDOW_LENGTH :], values[rows - WINDOW_LENGTH :], 0, kv_heads)
    rim = lax.ppermute(tail, "ctx", [(i, i + 1) for i in range(ctx - 1)])
    absent = jnp.where(lax.axis_index("ctx") == 0, WINDOW_LENGTH, 0).astype(jnp.int32)
    both = jnp.concatenate([rim, head_parts(keys, values, 0, kv_heads)], 2)
    both_grads = jnp.zeros(both.shape, jnp.float32)
    outs, query_grads = [], []
    for start in range(0, rows, BLOCK):
        here = slice(start, start + BLOCK)
        before = [both[:, :, at : at + BLOCK] for at in range(start, start + WINDOW_LENGTH, BLOCK)]
        o, dq, *parts = attention(
            jnp.maximum(absent - start, 0).reshape(1), queries[here], grads[here], keys[here], values[here],
            before, 0, kv_heads, None,
        )
        outs.append(o)
        query_grads.append(dq)
        for n, x in enumerate(parts):
            at = start + n * BLOCK
            both_grads = both_grads.at[:, :, at : at + BLOCK].add(wide(x))
    back = lax.ppermute(both_grads[:, :, :WINDOW_LENGTH], "ctx", [(i + 1, i) for i in range(ctx - 1)])
    own = both_grads[:, :, WINDOW_LENGTH:]
    own = own.at[:, :, rows - WINDOW_LENGTH :].add(back).astype(jnp.bfloat16)
    results = (jnp.concatenate(outs), jnp.concatenate(query_grads), side_by_side(own[:, 0]), side_by_side(own[:, 1]))
    return tuple(map(returned, results))


def on_device(queries, keys, values, output_gradient):
    rows = queries.shape[0]
    if 2 * rows == WINDOW_LENGTH and lax.axis_size(AXES) % 2 == 0:
        return by_tokens(queries, keys, values, output_gradient)
    return by_heads(queries, keys, values, output_gradient)


def solution(mesh):
    spec = P(AXES, None)
    return jax.shard_map(
        on_device, mesh=mesh, in_specs=(spec,) * 4, out_specs=(spec,) * 4, check_vma=False
    )
```

time: 98.5 us -> 76 us (0.77)
  starting transfers between devices: 37.4 us -> 20.5 us
  waiting for transfers between devices: 30.4 us -> 24.3 us
  other arithmetic: 2.79 us -> 6.46 us
  Pallas kernels: 24.4 us -> 21 us
  local copies, waits for them, and re-layouts: 1.41 us -> 2.7 us
    ppermute x24 -> x16, starting transfers between devices: 37.4 us -> 20.5 us  [the longest x4 7.79 us: fetch_far(): far[n] = lax.ppermute(block, AXES, ahead)]
    ppermute x24 -> x16, waiting for transfers between devices: 30.4 us -> 24.3 us  [the longest x4 8.95 us: give_far(): far_back[n] = lax.ppermute(relay[n], AXES, back)]
    pallas_call x4, Pallas kernels: 24.4 us -> 21 us  [attention(): pl.pallas_call(body, grid=(heads,), in_specs=in_specs, out_specs=out_spec...]
    another operation x4, other arithmetic: 0.11 us -> 2.21 us  [head_parts(): return both.transpose(2, 0, 1, 3)]
    select_n x4, other arithmetic: 0.14 us -> 1.75 us  [fetch_near(): send[n] = jnp.where(odd, far[n], mine[n])]
    unnamed x8 -> x10, local copies, waits for them, and re-layouts: 0.02 us -> 1.24 us
  transfers between devices with their start and end apart: 24 -> 16, of which waited for: 12 -> 7; matrix products, arithmetic and copies ran while one was open for 2% -> 6% of each run, Pallas kernels for 25% -> 28%
where the time goes in v1:
time: 76 us; the launch traced here: 75.8 us
  waiting for transfers between devices  24.3 us (32%)
  Pallas kernels  21 us (28%)
  starting transfers between devices  20.5 us (27%)
  other arithmetic  6.46 us (8%)
  local copies, waits for them, and re-layouts  2.7 us (4%)
  between operations  0.78 us (1%)
    pallas_call x4, Pallas kernels, attention(): pl.pallas_call(body, grid=(heads,), in_specs=in_specs, out_specs=out_spec...  21 us
    ppermute x4, waiting for transfers between devices, give_far(): far_back[n] = lax.ppermute(relay[n], AXES, back)  8.95 us
    ppermute x4, waiting for transfers between devices, give_near(): near_back[n] = lax.ppermute(to_near[n], AXES, swap)  8.43 us
    ppermute x4, starting transfers between devices, fetch_far(): far[n] = lax.ppermute(block, AXES, ahead)  7.79 us
    ppermute x4, starting transfers between devices, fetch_near(): near[n] = lax.ppermute(send[n], AXES, swap)  5.1 us
    ppermute x4, waiting for transfers between devices, fetch_far(): far[n] = lax.ppermute(block, AXES, ahead)  4.72 us
    ppermute x4, starting transfers between devices, give_far(): far_back[n] = lax.ppermute(relay[n], AXES, back)  4.25 us
    ppermute x4, starting transfers between devices, give_near(): near_back[n] = lax.ppermute(to_near[n], AXES, swap)  3.38 us
  transfers between devices with their start and end apart: 16, of which 7 were waited for; matrix products, arithmetic and copies ran while one was open for 6% of the time, Pallas kernels for 28%

profile of v1, /device:TPU:0, one launch (start us, length us, event | category | flops | bytes accessed | tf_op | source)
XLA Modules:
  0.0 75.8 jit_solution(14004899753424445348)
XLA Ops:
  0.6 1.4 %slice_bitcast_fusion.8 = (bf16[1,512,128]{2,1,0:T(8,128)(2,1)S(1)}, bf16[1,512,128]{2,1,0:T(8,128)(2,1)S(1)}, bf16[1,512,128]{2,1,0:T(8,128)(2,1)S(1)}, bf16[1,...) fusion(bf16[512,512]{1,0:T(8,128)(2,1)} %refs_8_.5, ...), kind=kLoop, calls=%fused_computation.38 | loop fusion | bytes 2097152 | tf_op jit(solution)/shard_map/stack | solution.py:214
  2.1 3.0 %collective-permute-start.1 = (bf16[1,2,512,128]{3,2,1,0:T(8,128)(2,1)S(1)}, bf16[1,2,512,128]{3,2,1,0:T(8,128)(2,1)S(1)}, u32[]{:S(2)}, u32[]{:S(2)}) collective-permute-start(bf16[1,2,512,128]{3,2,1,0:T(8,128)(2,1)S(1)} %maximum_bitcast_fusion.1), channel_id=1, source_target_pairs={{0,2},{1,3},{2,4},{3,5},{4,6},{5,7},{6,8},{7,9},{8,10},{9,11},{10,... | collective-permute-start | bytes 786440 | tf_op jit(solution)/shard_map/ppermute | solution.py:251
  7.1 4.7 %collective-permute-done.1.refs_0_.refs_1_ = bf16[1,2,512,128]{3,2,1,0:T(8,128)(2,1)S(1)} collective-permute-done((bf16[1,2,512,128]{3,2,1,0:T(8,128)(2,1)S(1)}, bf16[1,2,512,128]{3,2,1,0:T(8,128)(2,1)S(1)}, u32[]{:S(2)}, u32[]{:S(2)}) %collective-permute-start.1) | collective-permute-done | bytes 262176 | tf_op jit(solution)/shard_map/ppermute | solution.py:251
  12.5 1.9 %collective-permute-start.2 = (bf16[1,2,512,128]{3,2,1,0:T(8,128)(2,1)}, bf16[1,2,512,128]{3,2,1,0:T(8,128)(2,1)S(1)}, u32[]{:S(2)}, u32[]{:S(2)}) collective-permute-start(bf16[1,2,512,128]{3,2,1,0:T(8,128)(2,1)} %broadcast_select_fusion.2), channel_id=1, source_target_pairs={{0,1},{1,0},{2,3},{3,2},{4,5},{5,4},{6,7},{7,6},{8,9},{9,8},{10,11... | collective-permute-start | bytes 786440 | tf_op jit(solution)/shard_map/ppermute | solution.py:255
  15.1 2.1 %collective-permute-start.5 = (bf16[1,2,512,128]{3,2,1,0:T(8,128)(2,1)}, bf16[1,2,512,128]{3,2,1,0:T(8,128)(2,1)S(1)}, u32[]{:S(2)}, u32[]{:S(2)}) collective-permute-start(bf16[1,2,512,128]{3,2,1,0:T(8,128)(2,1)} %maximum_bitcast_fusion.3), channel_id=1, source_target_pairs={{0,2},{1,3},{2,4},{3,5},{4,6},{5,7},{6,8},{7,9},{8,10},{9,11},{10,... | collective-permute-start | bytes 786440 | tf_op jit(solution)/shard_map/ppermute | solution.py:251
  18.2 1.0 %collective-permute-start.6 = (bf16[1,2,512,128]{3,2,1,0:T(8,128)(2,1)S(1)}, bf16[1,2,512,128]{3,2,1,0:T(8,128)(2,1)S(1)}, u32[]{:S(2)}, u32[]{:S(2)}) collective-permute-start(bf16[1,2,512,128]{3,2,1,0:T(8,128)(2,1)S(1)} %broadcast_select_fusion.3), channel_id=1, source_target_pairs={{0,1},{1,0},{2,3},{3,2},{4,5},{5,4},{6,7},{7,6},{8,9},{9,8},{10,11... | collective-permute-start | bytes 786440 | tf_op jit(solution)/shard_map/ppermute | solution.py:255
  19.2 2.1 %collective-permute-start.4 = (bf16[1,2,512,128]{3,2,1,0:T(8,128)(2,1)}, bf16[1,2,512,128]{3,2,1,0:T(8,128)(2,1)S(1)}, u32[]{:S(2)}, u32[]{:S(2)}) collective-permute-start(bf16[1,2,512,128]{3,2,1,0:T(8,128)(2,1)} %maximum_bitcast_fusion.2), channel_id=1, source_target_pairs={{0,2},{1,3},{2,4},{3,5},{4,6},{5,7},{6,8},{7,9},{8,10},{9,11},{10,... | collective-permute-start | bytes 786440 | tf_op jit(solution)/shard_map/ppermute | solution.py:251
  21.3 1.2 %copy-done.3 = bf16[512,1024]{1,0:T(8,128)(2,1)S(1)} copy-done((bf16[512,1024]{1,0:T(8,128)(2,1)S(1)}, bf16[512,1024]{1,0:T(8,128)(2,1)}, u32[]{:S(2)}) %copy-start.3) | copy-done | bytes 1048600
  22.5 5.2 %attention.4 = (bf16[512,1024]{1,0:T(8,128)(2,1)}, bf16[512,1024]{1,0:T(8,128)(2,1)}, bf16[1,2,512,128]{3,2,1,0:T(8,128)(2,1)S(1)}, bf16[1,2,512,128]{3,2,1,0:T(8,128)(2,1)S(1)}, f32[1,2,512,128]{3,2,1,0:T(8,128)S(1)}) custom-call(s32[1]{0:T(128)} %bitcast.absent_ref.refs_0_, bf16[512,1024]{1,0:T(8,128)(2,1)S(1)} %copy-done.2, ...), custom_call_target="tpu_custom_call" | custom-call | flops 2013265920 | bytes 2097152 | tf_op jit(solution)/shard_map/attention/pallas_call | solution.py:185
  27.8 1.1 %collective-permute-start.7 = (bf16[1,2,512,128]{3,2,1,0:T(8,128)(2,1)S(1)}, bf16[1,2,512,128]{3,2,1,0:T(8,128)(2,1)S(1)}, u32[]{:S(2)}, u32[]{:S(2)}) collective-permute-start(bf16[1,2,512,128]{3,2,1,0:T(8,128)(2,1)S(1)} %broadcast_select_fusion.1), channel_id=1, source_target_pairs={{0,1},{1,0},{2,3},{3,2},{4,5},{5,4},{6,7},{7,6},{8,9},{9,8},{10,11... | collective-permute-start | bytes 786440 | tf_op jit(solution)/shard_map/ppermute | solution.py:255
  29.9 5.2 %attention.5 = (bf16[512,1024]{1,0:T(8,128)(2,1)}, bf16[512,1024]{1,0:T(8,128)(2,1)}, bf16[1,2,512,128]{3,2,1,0:T(8,128)(2,1)S(1)}, bf16[1,2,512,128]{3,2,1,0:T(8,128)(2,1)S(1)}, f32[1,2,512,128]{3,2,1,0:T(8,128)S(1)}) custom-call(s32[1]{0:T(128)} %bitcast.absent_ref.refs_0_, ...), custom_call_target="tpu_custom_call", output_to_operand_aliasing={{0}: (9, {}), {1}: (10, {})} | custom-call | flops 2013265920 | bytes 2097152 | tf_op jit(solution)/shard_map/attention/pallas_call | solution.py:185
  35.1 1.1 %collective-permute-start.8 = (bf16[1,2,512,128]{3,2,1,0:T(8,128)(2,1)S(1)}, bf16[1,2,512,128]{3,2,1,0:T(8,128)(2,1)S(1)}, u32[]{:S(2)}, u32[]{:S(2)}) collective-permute-start(bf16[1,2,512,128]{3,2,1,0:T(8,128)(2,1)S(1)} %broadcast_select_fusion), channel_id=1, source_target_pairs={{0,1},{1,0},{2,3},{3,2},{4,5},{5,4},{6,7},{7,6},{8,9},{9,8},{10,11... | collective-permute-start | bytes 786440 | tf_op jit(solution)/shard_map/ppermute | solution.py:255
  36.2 0.9 %collective-permute-start.10 = (bf16[1,2,512,128]{3,2,1,0:T(8,128)(2,1)S(1)}, bf16[1,2,512,128]{3,2,1,0:T(8,128)(2,1)S(1)}, u32[]{:S(2)}, u32[]{:S(2)}) collective-permute-start(bf16[1,2,512,128]{3,2,1,0:T(8,128)(2,1)S(1)} %get-tuple-element.57), channel_id=1, source_target_pairs={{0,1},{1,0},{2,3},{3,2},{4,5},{5,4},{6,7},{7,6},{8,9},{9,8},{10,11... | collective-permute-start | bytes 786440 | tf_op jit(solution)/shard_map/ppermute | solution.py:258
  37.2 5.4 %attention.6 = (bf16[512,1024]{1,0:T(8,128)(2,1)}, bf16[512,1024]{1,0:T(8,128)(2,1)}, bf16[1,2,512,128]{3,2,1,0:T(8,128)(2,1)S(1)}, bf16[1,2,512,128]{3,2,1,0:T(8,128)(2,1)S(1)}, f32[1,2,512,128]{3,2,1,0:T(8,128)S(1)}) custom-call(s32[1]{0:T(128)} %bitcast.absent_ref.refs_0_, ...), custom_call_target="tpu_custom_call", output_to_operand_aliasing={{0}: (9, {}), {1}: (10, {})} | custom-call | flops 2013265920 | bytes 2097152 | tf_op jit(solution)/shard_map/attention/pallas_call | solution.py:185
  42.7 1.3 %collective-permute-start.9 = (bf16[1,2,512,128]{3,2,1,0:T(8,128)(2,1)S(1)}, bf16[1,2,512,128]{3,2,1,0:T(8,128)(2,1)S(1)}, u32[]{:S(2)}, u32[]{:S(2)}) collective-permute-start(bf16[1,2,512,128]{3,2,1,0:T(8,128)(2,1)S(1)} %fusion.8), channel_id=1, source_target_pairs={{2,0},{3,1},{4,2},{5,3},{6,4},{7,5},{8,6},{9,7},{10,8},{11,9},{12,... | collective-permute-start | bytes 786440 | tf_op jit(solution)/shard_map/ppermute | solution.py:262
  43.9 1.1 %collective-permute-start.12 = (bf16[1,2,512,128]{3,2,1,0:T(8,128)(2,1)S(1)}, bf16[1,2,512,128]{3,2,1,0:T(8,128)(2,1)S(1)}, u32[]{:S(2)}, u32[]{:S(2)}) collective-permute-start(bf16[1,2,512,128]{3,2,1,0:T(8,128)(2,1)S(1)} %get-tuple-element.61), channel_id=1, source_target_pairs={{0,1},{1,0},{2,3},{3,2},{4,5},{5,4},{6,7},{7,6},{8,9},{9,8},{10,11... | collective-permute-start | bytes 786440 | tf_op jit(solution)/shard_map/ppermute | solution.py:258
  45.1 2.2 %collective-permute-done.8.refs_5_.refs_6_ = bf16[1,2,512,128]{3,2,1,0:T(8,128)(2,1)S(1)} collective-permute-done((bf16[1,2,512,128]{3,2,1,0:T(8,128)(2,1)S(1)}, bf16[1,2,512,128]{3,2,1,0:T(8,128)(2,1)S(1)}, u32[]{:S(2)}, u32[]{:S(2)}) %collective-permute-start.8) | collective-permute-done | bytes 262176 | tf_op jit(solution)/shard_map/ppermute | solution.py:255
  47.3 5.2 %attention.7 = (bf16[512,1024]{1,0:T(8,128)(2,1)}, bf16[512,1024]{1,0:T(8,128)(2,1)}, bf16[1,2,512,128]{3,2,1,0:T(8,128)(2,1)S(1)}, bf16[1,2,512,128]{3,2,1,0:T(8,128)(2,1)S(1)}, f32[1,2,512,128]{3,2,1,0:T(8,128)S(1)}) custom-call(s32[1]{0:T(128)} %bitcast.absent_ref.refs_0_, ...), custom_call_target="tpu_custom_call", output_to_operand_aliasing={{0}: (9, {}), {1}: (10, {})} | custom-call | flops 2013265920 | bytes 2097152 | tf_op jit(solution)/shard_map/attention/pallas_call | solution.py:185
  53.4 1.0 %collective-permute-start.11 = (bf16[1,2,512,128]{3,2,1,0:T(8,128)(2,1)S(1)}, bf16[1,2,512,128]{3,2,1,0:T(8,128)(2,1)S(1)}, u32[]{:S(2)}, u32[]{:S(2)}) collective-permute-start(bf16[1,2,512,128]{3,2,1,0:T(8,128)(2,1)S(1)} %fusion.9), channel_id=1, source_target_pairs={{2,0},{3,1},{4,2},{5,3},{6,4},{7,5},{8,6},{9,7},{10,8},{11,9},{12,... | collective-permute-start | bytes 786440 | tf_op jit(solution)/shard_map/ppermute | solution.py:262
  54.4 4.2 %collective-permute-done.12 = bf16[1,2,512,128]{3,2,1,0:T(8,128)(2,1)S(1)} collective-permute-done((bf16[1,2,512,128]{3,2,1,0:T(8,128)(2,1)S(1)}, bf16[1,2,512,128]{3,2,1,0:T(8,128)(2,1)S(1)}, u32[]{:S(2)}, u32[]{:S(2)}) %collective-permute-start.12) | collective-permute-done | bytes 262176 | tf_op jit(solution)/shard_map/ppermute | solution.py:258
  58.7 1.7 %collective-permute-start.13 = (bf16[1,2,512,128]{3,2,1,0:T(8,128)(2,1)S(1)}, bf16[1,2,512,128]{3,2,1,0:T(8,128)(2,1)S(1)}, u32[]{:S(2)}, u32[]{:S(2)}) collective-permute-start(bf16[1,2,512,128]{3,2,1,0:T(8,128)(2,1)S(1)} %fusion.10), channel_id=1, source_target_pairs={{2,0},{3,1},{4,2},{5,3},{6,4},{7,5},{8,6},{9,7},{10,8},{11,9},{12,... | collective-permute-start | bytes 786440 | tf_op jit(solution)/shard_map/ppermute | solution.py:262
  60.4 3.8 %collective-permute-done.14 = bf16[1,2,512,128]{3,2,1,0:T(8,128)(2,1)S(1)} collective-permute-done((bf16[1,2,512,128]{3,2,1,0:T(8,128)(2,1)S(1)}, bf16[1,2,512,128]{3,2,1,0:T(8,128)(2,1)S(1)}, u32[]{:S(2)}, u32[]{:S(2)}) %collective-permute-start.14) | collective-permute-done | bytes 262176 | tf_op jit(solution)/shard_map/ppermute | solution.py:258
  64.8 3.5 %collective-permute-done.13 = bf16[1,2,512,128]{3,2,1,0:T(8,128)(2,1)S(1)} collective-permute-done((bf16[1,2,512,128]{3,2,1,0:T(8,128)(2,1)S(1)}, bf16[1,2,512,128]{3,2,1,0:T(8,128)(2,1)S(1)}, u32[]{:S(2)}, u32[]{:S(2)}) %collective-permute-start.13) | collective-permute-done | bytes 262176 | tf_op jit(solution)/shard_map/ppermute | solution.py:262
  68.4 5.5 %collective-permute-done.15 = bf16[1,2,512,128]{3,2,1,0:T(8,128)(2,1)S(1)} collective-permute-done((bf16[1,2,512,128]{3,2,1,0:T(8,128)(2,1)S(1)}, bf16[1,2,512,128]{3,2,1,0:T(8,128)(2,1)S(1)}, u32[]{:S(2)}, u32[]{:S(2)}) %collective-permute-start.15) | collective-permute-done | bytes 262176 | tf_op jit(solution)/shard_map/ppermute | solution.py:262
  (45 shorter events, 9.1 us)
Async XLA Ops:
  2.0 3.1 %copy-start.4 = (bf16[1,512,128]{2,1,0:T(8,128)(2,1)}, bf16[1,512,128]{2,1,0:T(8,128)(2,1)S(1)}, u32[]{:S(2)}) copy-start(bf16[1,512,128]{2,1,0:T(8,128)(2,1)S(1)} %get-tuple-element.80) | copy-start | bytes 393220
  2.1 9.7 %collective-permute-start.1 = (bf16[1,2,512,128]{3,2,1,0:T(8,128)(2,1)S(1)}, bf16[1,2,512,128]{3,2,1,0:T(8,128)(2,1)S(1)}, u32[]{:S(2)}, u32[]{:S(2)}) collective-permute-start(bf16[1,2,512,128]{3,2,1,0:T(8,128)(2,1)S(1)} %maximum_bitcast_fusion.1), channel_id=1, source_target_pairs={{0,2},{1,3},{2,4},{3,5},{4,6},{5,7},{6,8},{7,9},{8,10},{9,11},{10,... | collective-permute-start | bytes 786440 | tf_op jit(solution)/shard_map/ppermute | solution.py:251
  5.8 11.4 %collective-permute-start = (bf16[1,2,512,128]{3,2,1,0:T(8,128)(2,1)}, bf16[1,2,512,128]{3,2,1,0:T(8,128)(2,1)S(1)}, u32[]{:S(2)}, u32[]{:S(2)}) collective-permute-start(bf16[1,2,512,128]{3,2,1,0:T(8,128)(2,1)} %maximum_bitcast_fusion), channel_id=1, source_target_pairs={{0,2},{1,3},{2,4},{3,5},{4,6},{5,7},{6,8},{7,9},{8,10},{9,11},{10,... | collective-permute-start | bytes 786440 | tf_op jit(solution)/shard_map/ppermute | solution.py:251
  7.1 14.2 %copy-start.2 = (bf16[512,1024]{1,0:T(8,128)(2,1)S(1)}, bf16[512,1024]{1,0:T(8,128)(2,1)}, u32[]{:S(2)}) copy-start(bf16[512,1024]{1,0:T(8,128)(2,1)} %refs_1_.5) | copy-start | bytes 3145732
  12.5 8.7 %collective-permute-start.2 = (bf16[1,2,512,128]{3,2,1,0:T(8,128)(2,1)}, bf16[1,2,512,128]{3,2,1,0:T(8,128)(2,1)S(1)}, u32[]{:S(2)}, u32[]{:S(2)}) collective-permute-start(bf16[1,2,512,128]{3,2,1,0:T(8,128)(2,1)} %broadcast_select_fusion.2), channel_id=1, source_target_pairs={{0,1},{1,0},{2,3},{3,2},{4,5},{5,4},{6,7},{7,6},{8,9},{9,8},{10,11... | collective-permute-start | bytes 786440 | tf_op jit(solution)/shard_map/ppermute | solution.py:255
  14.4 6.9 %copy-start.1 = (bf16[512,512]{1,0:T(8,128)(2,1)S(1)}, bf16[512,512]{1,0:T(8,128)(2,1)}, u32[]{:S(2)}) copy-start(bf16[512,512]{1,0:T(8,128)(2,1)} %refs_7_.5) | copy-start | bytes 1572868
  15.1 6.1 %copy-start = (bf16[512,512]{1,0:T(8,128)(2,1)S(1)}, bf16[512,512]{1,0:T(8,128)(2,1)}, u32[]{:S(2)}) copy-start(bf16[512,512]{1,0:T(8,128)(2,1)} %refs_8_.5) | copy-start | bytes 1572868
  15.1 12.6 %collective-permute-start.5 = (bf16[1,2,512,128]{3,2,1,0:T(8,128)(2,1)}, bf16[1,2,512,128]{3,2,1,0:T(8,128)(2,1)S(1)}, u32[]{:S(2)}, u32[]{:S(2)}) collective-permute-start(bf16[1,2,512,128]{3,2,1,0:T(8,128)(2,1)} %maximum_bitcast_fusion.3), channel_id=1, source_target_pairs={{0,2},{1,3},{2,4},{3,5},{4,6},{5,7},{6,8},{7,9},{8,10},{9,11},{10,... | collective-permute-start | bytes 786440 | tf_op jit(solution)/shard_map/ppermute | solution.py:251
  18.2 11.7 %collective-permute-start.6 = (bf16[1,2,512,128]{3,2,1,0:T(8,128)(2,1)S(1)}, bf16[1,2,512,128]{3,2,1,0:T(8,128)(2,1)S(1)}, u32[]{:S(2)}, u32[]{:S(2)}) collective-permute-start(bf16[1,2,512,128]{3,2,1,0:T(8,128)(2,1)S(1)} %broadcast_select_fusion.3), channel_id=1, source_target_pairs={{0,1},{1,0},{2,3},{3,2},{4,5},{5,4},{6,7},{7,6},{8,9},{9,8},{10,11... | collective-permute-start | bytes 786440 | tf_op jit(solution)/shard_map/ppermute | solution.py:255
  19.2 15.9 %collective-permute-start.4 = (bf16[1,2,512,128]{3,2,1,0:T(8,128)(2,1)}, bf16[1,2,512,128]{3,2,1,0:T(8,128)(2,1)S(1)}, u32[]{:S(2)}, u32[]{:S(2)}) collective-permute-start(bf16[1,2,512,128]{3,2,1,0:T(8,128)(2,1)} %maximum_bitcast_fusion.2), channel_id=1, source_target_pairs={{0,2},{1,3},{2,4},{3,5},{4,6},{5,7},{6,8},{7,9},{8,10},{9,11},{10,... | collective-permute-start | bytes 786440 | tf_op jit(solution)/shard_map/ppermute | solution.py:251
  21.3 1.2 %copy-start.3 = (bf16[512,1024]{1,0:T(8,128)(2,1)S(1)}, bf16[512,1024]{1,0:T(8,128)(2,1)}, u32[]{:S(2)}) copy-start(bf16[512,1024]{1,0:T(8,128)(2,1)} %refs_2_.5) | copy-start | bytes 3145732
  27.8 9.4 %collective-permute-start.7 = (bf16[1,2,512,128]{3,2,1,0:T(8,128)(2,1)S(1)}, bf16[1,2,512,128]{3,2,1,0:T(8,128)(2,1)S(1)}, u32[]{:S(2)}, u32[]{:S(2)}) collective-permute-start(bf16[1,2,512,128]{3,2,1,0:T(8,128)(2,1)S(1)} %broadcast_select_fusion.1), channel_id=1, source_target_pairs={{0,1},{1,0},{2,3},{3,2},{4,5},{5,4},{6,7},{7,6},{8,9},{9,8},{10,11... | collective-permute-start | bytes 786440 | tf_op jit(solution)/shard_map/ppermute | solution.py:255
  28.9 13.7 %collective-permute-start.3 = (bf16[1,2,512,128]{3,2,1,0:T(8,128)(2,1)S(1)}, bf16[1,2,512,128]{3,2,1,0:T(8,128)(2,1)S(1)}, u32[]{:S(2)}, u32[]{:S(2)}) collective-permute-start(bf16[1,2,512,128]{3,2,1,0:T(8,128)(2,1)S(1)} %get-tuple-element.36), channel_id=1, source_target_pairs={{0,1},{1,0},{2,3},{3,2},{4,5},{5,4},{6,7},{7,6},{8,9},{9,8},{10,11... | collective-permute-start | bytes 786440 | tf_op jit(solution)/shard_map/ppermute | solution.py:258
  35.1 12.2 %collective-permute-start.8 = (bf16[1,2,512,128]{3,2,1,0:T(8,128)(2,1)S(1)}, bf16[1,2,512,128]{3,2,1,0:T(8,128)(2,1)S(1)}, u32[]{:S(2)}, u32[]{:S(2)}) collective-permute-start(bf16[1,2,512,128]{3,2,1,0:T(8,128)(2,1)S(1)} %broadcast_select_fusion), channel_id=1, source_target_pairs={{0,1},{1,0},{2,3},{3,2},{4,5},{5,4},{6,7},{7,6},{8,9},{9,8},{10,11... | collective-permute-start | bytes 786440 | tf_op jit(solution)/shard_map/ppermute | solution.py:255
  36.2 16.7 %collective-permute-start.10 = (bf16[1,2,512,128]{3,2,1,0:T(8,128)(2,1)S(1)}, bf16[1,2,512,128]{3,2,1,0:T(8,128)(2,1)S(1)}, u32[]{:S(2)}, u32[]{:S(2)}) collective-permute-start(bf16[1,2,512,128]{3,2,1,0:T(8,128)(2,1)S(1)} %get-tuple-element.57), channel_id=1, source_target_pairs={{0,1},{1,0},{2,3},{3,2},{4,5},{5,4},{6,7},{7,6},{8,9},{9,8},{10,11... | collective-permute-start | bytes 786440 | tf_op jit(solution)/shard_map/ppermute | solution.py:258
  42.7 21.9 %collective-permute-start.9 = (bf16[1,2,512,128]{3,2,1,0:T(8,128)(2,1)S(1)}, bf16[1,2,512,128]{3,2,1,0:T(8,128)(2,1)S(1)}, u32[]{:S(2)}, u32[]{:S(2)}) collective-permute-start(bf16[1,2,512,128]{3,2,1,0:T(8,128)(2,1)S(1)} %fusion.8), channel_id=1, source_target_pairs={{2,0},{3,1},{4,2},{5,3},{6,4},{7,5},{8,6},{9,7},{10,8},{11,9},{12,... | collective-permute-start | bytes 786440 | tf_op jit(solution)/shard_map/ppermute | solution.py:262
  43.9 14.6 %collective-permute-start.12 = (bf16[1,2,512,128]{3,2,1,0:T(8,128)(2,1)S(1)}, bf16[1,2,512,128]{3,2,1,0:T(8,128)(2,1)S(1)}, u32[]{:S(2)}, u32[]{:S(2)}) collective-permute-start(bf16[1,2,512,128]{3,2,1,0:T(8,128)(2,1)S(1)} %get-tuple-element.61), channel_id=1, source_target_pairs={{0,1},{1,0},{2,3},{3,2},{4,5},{5,4},{6,7},{7,6},{8,9},{9,8},{10,11... | collective-permute-start | bytes 786440 | tf_op jit(solution)/shard_map/ppermute | solution.py:258
  52.9 11.2 %collective-permute-start.14 = (bf16[1,2,512,128]{3,2,1,0:T(8,128)(2,1)S(1)}, bf16[1,2,512,128]{3,2,1,0:T(8,128)(2,1)S(1)}, u32[]{:S(2)}, u32[]{:S(2)}) collective-permute-start(bf16[1,2,512,128]{3,2,1,0:T(8,128)(2,1)S(1)} %get-tuple-element.63), channel_id=1, source_target_pairs={{0,1},{1,0},{2,3},{3,2},{4,5},{5,4},{6,7},{7,6},{8,9},{9,8},{10,11... | collective-permute-start | bytes 786440 | tf_op jit(solution)/shard_map/ppermute | solution.py:258
  53.4 11.3 %collective-permute-start.11 = (bf16[1,2,512,128]{3,2,1,0:T(8,128)(2,1)S(1)}, bf16[1,2,512,128]{3,2,1,0:T(8,128)(2,1)S(1)}, u32[]{:S(2)}, u32[]{:S(2)}) collective-permute-start(bf16[1,2,512,128]{3,2,1,0:T(8,128)(2,1)S(1)} %fusion.9), channel_id=1, source_target_pairs={{2,0},{3,1},{4,2},{5,3},{6,4},{7,5},{8,6},{9,7},{10,8},{11,9},{12,... | collective-permute-start | bytes 786440 | tf_op jit(solution)/shard_map/ppermute | solution.py:262
  58.7 9.6 %collective-permute-start.13 = (bf16[1,2,512,128]{3,2,1,0:T(8,128)(2,1)S(1)}, bf16[1,2,512,128]{3,2,1,0:T(8,128)(2,1)S(1)}, u32[]{:S(2)}, u32[]{:S(2)}) collective-permute-start(bf16[1,2,512,128]{3,2,1,0:T(8,128)(2,1)S(1)} %fusion.10), channel_id=1, source_target_pairs={{2,0},{3,1},{4,2},{5,3},{6,4},{7,5},{8,6},{9,7},{10,8},{11,9},{12,... | collective-permute-start | bytes 786440 | tf_op jit(solution)/shard_map/ppermute | solution.py:262
  64.3 9.6 %collective-permute-start.15 = (bf16[1,2,512,128]{3,2,1,0:T(8,128)(2,1)S(1)}, bf16[1,2,512,128]{3,2,1,0:T(8,128)(2,1)S(1)}, u32[]{:S(2)}, u32[]{:S(2)}) collective-permute-start(bf16[1,2,512,128]{3,2,1,0:T(8,128)(2,1)S(1)} %fusion.11), channel_id=1, source_target_pairs={{2,0},{3,1},{4,2},{5,3},{6,4},{7,5},{8,6},{9,7},{10,8},{11,9},{12,... | collective-permute-start | bytes 786440 | tf_op jit(solution)/shard_map/ppermute | solution.py:262

commit v2 on v1

--- a/solution.py
+++ b/solution.py
@@ -211,6 +211,8 @@
 def head_parts(keys, values, head, heads):
     rows = keys.shape[0]
     span = slice(head * HEAD_SIZE, (head + heads) * HEAD_SIZE)
+    if heads == 1:
+        return jnp.stack([lax.optimization_barrier(keys[:, span]), lax.optimization_barrier(values[:, span])], 0)[None]
     both = jnp.stack([keys[:, span], values[:, span]], 0).reshape(2, rows, heads, HEAD_SIZE)
     return both.transpose(2, 0, 1, 3)
 
@@ -258,6 +260,8 @@
         near_back[n] = lax.ppermute(to_near[n], AXES, swap)
 
     def give_far(n):
+        if n > 0:
+            near_back[n] = after(near_back[n], relay[n - 1])
         relay[n] = jnp.where(odd, wide(to_far[n]) + wide(near_back[n]), wide(to_far[n])).astype(jnp.bfloat16)
         far_back[n] = lax.ppermute(relay[n], AXES, back)
 
@@ -277,17 +281,18 @@
     held[2] = (send[0],)
     fetch_far(2)
     fetch_near(1)
-    held[3] = (far[1],)
+    held[3] = (send[1],)
     fetch_far(3)
     compute(0, send[1])
     give_near(0)
     far[2] = after(far[2], to_far[0])
     fetch_near(2)
     compute(1, send[2])
-    give_near(1)
     far[3] = after(far[3], to_far[1])
     fetch_near(3)
     compute(2, send[3])
+    to_near[1] = after(to_near[1], to_far[2])
+    give_near(1)
     give_near(2)
     near_back[0] = after(near_back[0], to_far[2])
     give_far(0)

time: 76 us -> 75.1 us (0.988)
  waiting for transfers between devices: 24.3 us -> 22.8 us
  starting transfers between devices: 20.5 us -> 21.9 us
    broadcast_in_dim x0 -> x4, other arithmetic: none -> 2.21 us  [head_parts(): jnp.stack([lax.optimization_barrier(keys[:, span]), lax.optimization_barr...]
    another operation x4 -> x0, other arithmetic: 2.21 us -> none  [head_parts(): return both.transpose(2, 0, 1, 3)]
    ppermute x4, starting transfers between devices: 4.25 us -> 5.66 us  [give_far(): far_back[n] = lax.ppermute(relay[n], AXES, back)]
    another operation x1 -> x0, local copies, waits for them, and re-layouts: 1.39 us -> none  [head_parts(): jnp.stack([keys[:, span], values[:, span]], 0)]
    ppermute x4, waiting for transfers between devices: 8.43 us -> 7.1 us  [give_near(): near_back[n] = lax.ppermute(to_near[n], AXES, swap)]
    slice x0 -> x2, local copies, waits for them, and re-layouts: none -> 1.29 us  [the longest x1 1.2 us: head_parts(): keys[:, span]]
    concatenate x1 -> x0, other arithmetic: 0.86 us -> none  [by_tokens(): jnp.concatenate(value_grads, 1)]
  transfers between devices with their start and end apart: 16 -> 16, of which waited for: 7 -> 8; matrix products, arithmetic and copies ran while one was open for 6% -> 6% of each run, Pallas kernels for 28% -> 28%
where the time goes in v2:
time: 75.1 us; the launch traced here: 74.9 us
  waiting for transfers between devices  22.8 us (30%)
  starting transfers between devices  21.9 us (29%)
  Pallas kernels  21 us (28%)
  other arithmetic  5.82 us (8%)
  local copies, waits for them, and re-layouts  2.7 us (4%)
  between operations  0.79 us (1%)
    pallas_call x4, Pallas kernels, attention(): pl.pallas_call(body, grid=(heads,), in_specs=in_specs, out_specs=out_spec...  21 us
    ppermute x4, waiting for transfers between devices, give_far(): far_back[n] = lax.ppermute(relay[n], AXES, back)  8.75 us
    ppermute x4, starting transfers between devices, fetch_far(): far[n] = lax.ppermute(block, AXES, ahead)  7.79 us
    ppermute x4, waiting for transfers between devices, give_near(): near_back[n] = lax.ppermute(to_near[n], AXES, swap)  7.1 us
    ppermute x4, starting transfers between devices, give_far(): far_back[n] = lax.ppermute(relay[n], AXES, back)  5.66 us
    ppermute x4, starting transfers between devices, fetch_near(): near[n] = lax.ppermute(send[n], AXES, swap)  5.1 us
    ppermute x4, waiting for transfers between devices, fetch_far(): far[n] = lax.ppermute(block, AXES, ahead)  4.72 us
    ppermute x4, starting transfers between devices, give_near(): near_back[n] = lax.ppermute(to_near[n], AXES, swap)  3.33 us
  transfers between devices with their start and end apart: 16, of which 8 were waited for; matrix products, arithmetic and copies ran while one was open for 6% of the time, Pallas kernels for 28%

profile of v2, /device:TPU:0, one launch (start us, length us, event | category | flops | bytes accessed | tf_op | source)
XLA Modules:
  0.0 74.9 jit_solution(15429591403473126446)
XLA Ops:
  0.6 1.2 %fusion.12 = (bf16[512,128]{1,0:T(8,128)(2,1)S(1)}, bf16[512,128]{1,0:T(8,128)(2,1)S(1)}, bf16[512,128]{1,0:T(8,128)(2,1)S(1)}, bf16[512,128]{1,0:T(8,128)(2,1)S(1)}) fusion(bf16[512,512]{1,0:T(8,128)(2,1)} %refs_7_.5), kind=kLoop, calls=%fused_computation.38 | loop fusion | bytes 1048576 | tf_op jit(solution)/shard_map/slice | solution.py:215
  2.1 3.0 %collective-permute-start.1 = (bf16[1,2,512,128]{3,2,1,0:T(8,128)(2,1)S(1)}, bf16[1,2,512,128]{3,2,1,0:T(8,128)(2,1)S(1)}, u32[]{:S(2)}, u32[]{:S(2)}) collective-permute-start(bf16[1,2,512,128]{3,2,1,0:T(8,128)(2,1)S(1)} %maximum_bitcast_fusion.1), channel_id=1, source_target_pairs={{0,2},{1,3},{2,4},{3,5},{4,6},{5,7},{6,8},{7,9},{8,10},{9,11},{10,... | collective-permute-start | bytes 786440 | tf_op jit(solution)/shard_map/ppermute | solution.py:253
  7.1 4.7 %collective-permute-done.1.refs_0_.refs_1_ = bf16[1,2,512,128]{3,2,1,0:T(8,128)(2,1)S(1)} collective-permute-done((bf16[1,2,512,128]{3,2,1,0:T(8,128)(2,1)S(1)}, bf16[1,2,512,128]{3,2,1,0:T(8,128)(2,1)S(1)}, u32[]{:S(2)}, u32[]{:S(2)}) %collective-permute-start.1) | collective-permute-done | bytes 262176 | tf_op jit(solution)/shard_map/ppermute | solution.py:253
  12.6 1.9 %collective-permute-start.2 = (bf16[1,2,512,128]{3,2,1,0:T(8,128)(2,1)}, bf16[1,2,512,128]{3,2,1,0:T(8,128)(2,1)S(1)}, u32[]{:S(2)}, u32[]{:S(2)}) collective-permute-start(bf16[1,2,512,128]{3,2,1,0:T(8,128)(2,1)} %broadcast_select_fusion.2), channel_id=1, source_target_pairs={{0,1},{1,0},{2,3},{3,2},{4,5},{5,4},{6,7},{7,6},{8,9},{9,8},{10,11... | collective-permute-start | bytes 786440 | tf_op jit(solution)/shard_map/ppermute | solution.py:257
  15.1 2.1 %collective-permute-start.5 = (bf16[1,2,512,128]{3,2,1,0:T(8,128)(2,1)}, bf16[1,2,512,128]{3,2,1,0:T(8,128)(2,1)S(1)}, u32[]{:S(2)}, u32[]{:S(2)}) collective-permute-start(bf16[1,2,512,128]{3,2,1,0:T(8,128)(2,1)} %maximum_bitcast_fusion.3), channel_id=1, source_target_pairs={{0,2},{1,3},{2,4},{3,5},{4,6},{5,7},{6,8},{7,9},{8,10},{9,11},{10,... | collective-permute-start | bytes 786440 | tf_op jit(solution)/shard_map/ppermute | solution.py:253
  18.2 1.0 %collective-permute-start.6 = (bf16[1,2,512,128]{3,2,1,0:T(8,128)(2,1)S(1)}, bf16[1,2,512,128]{3,2,1,0:T(8,128)(2,1)S(1)}, u32[]{:S(2)}, u32[]{:S(2)}) collective-permute-start(bf16[1,2,512,128]{3,2,1,0:T(8,128)(2,1)S(1)} %broadcast_select_fusion.3), channel_id=1, source_target_pairs={{0,1},{1,0},{2,3},{3,2},{4,5},{5,4},{6,7},{7,6},{8,9},{9,8},{10,11... | collective-permute-start | bytes 786440 | tf_op jit(solution)/shard_map/ppermute | solution.py:257
  19.2 2.1 %collective-permute-start.4 = (bf16[1,2,512,128]{3,2,1,0:T(8,128)(2,1)S(1)}, bf16[1,2,512,128]{3,2,1,0:T(8,128)(2,1)S(1)}, u32[]{:S(2)}, u32[]{:S(2)}) collective-permute-start(bf16[1,2,512,128]{3,2,1,0:T(8,128)(2,1)S(1)} %copy-done.6), channel_id=1, source_target_pairs={{0,2},{1,3},{2,4},{3,5},{4,6},{5,7},{6,8},{7,9},{8,10},{9,11},{10,... | collective-permute-start | bytes 786440 | tf_op jit(solution)/shard_map/ppermute | solution.py:253
  21.3 1.2 %copy-done.3 = bf16[512,1024]{1,0:T(8,128)(2,1)S(1)} copy-done((bf16[512,1024]{1,0:T(8,128)(2,1)S(1)}, bf16[512,1024]{1,0:T(8,128)(2,1)}, u32[]{:S(2)}) %copy-start.3) | copy-done | bytes 1048600
  22.5 5.2 %attention.4 = (bf16[512,1024]{1,0:T(8,128)(2,1)}, bf16[512,1024]{1,0:T(8,128)(2,1)}, bf16[1,2,512,128]{3,2,1,0:T(8,128)(2,1)S(1)}, bf16[1,2,512,128]{3,2,1,0:T(8,128)(2,1)S(1)}, f32[1,2,512,128]{3,2,1,0:T(8,128)S(1)}) custom-call(s32[1]{0:T(128)} %bitcast.absent_ref.refs_0_, bf16[512,1024]{1,0:T(8,128)(2,1)S(1)} %copy-done.2, ...), custom_call_target="tpu_custom_call" | custom-call | flops 2013265920 | bytes 2097152 | tf_op jit(solution)/shard_map/attention/pallas_call | solution.py:185
  27.8 1.1 %collective-permute-start.7 = (bf16[1,2,512,128]{3,2,1,0:T(8,128)(2,1)S(1)}, bf16[1,2,512,128]{3,2,1,0:T(8,128)(2,1)S(1)}, u32[]{:S(2)}, u32[]{:S(2)}) collective-permute-start(bf16[1,2,512,128]{3,2,1,0:T(8,128)(2,1)S(1)} %broadcast_select_fusion.1), channel_id=1, source_target_pairs={{0,1},{1,0},{2,3},{3,2},{4,5},{5,4},{6,7},{7,6},{8,9},{9,8},{10,11... | collective-permute-start | bytes 786440 | tf_op jit(solution)/shard_map/ppermute | solution.py:257
  29.9 5.2 %attention.5 = (bf16[512,1024]{1,0:T(8,128)(2,1)}, bf16[512,1024]{1,0:T(8,128)(2,1)}, bf16[1,2,512,128]{3,2,1,0:T(8,128)(2,1)S(1)}, bf16[1,2,512,128]{3,2,1,0:T(8,128)(2,1)S(1)}, f32[1,2,512,128]{3,2,1,0:T(8,128)S(1)}) custom-call(s32[1]{0:T(128)} %bitcast.absent_ref.refs_0_, ...), custom_call_target="tpu_custom_call", output_to_operand_aliasing={{0}: (9, {}), {1}: (10, {})} | custom-call | flops 2013265920 | bytes 2097152 | tf_op jit(solution)/shard_map/attention/pallas_call | solution.py:185
  35.1 1.1 %collective-permute-start.8 = (bf16[1,2,512,128]{3,2,1,0:T(8,128)(2,1)S(1)}, bf16[1,2,512,128]{3,2,1,0:T(8,128)(2,1)S(1)}, u32[]{:S(2)}, u32[]{:S(2)}) collective-permute-start(bf16[1,2,512,128]{3,2,1,0:T(8,128)(2,1)S(1)} %broadcast_select_fusion), channel_id=1, source_target_pairs={{0,1},{1,0},{2,3},{3,2},{4,5},{5,4},{6,7},{7,6},{8,9},{9,8},{10,11... | collective-permute-start | bytes 786440 | tf_op jit(solution)/shard_map/ppermute | solution.py:257
  36.2 5.4 %attention.6 = (bf16[512,1024]{1,0:T(8,128)(2,1)}, bf16[512,1024]{1,0:T(8,128)(2,1)}, bf16[1,2,512,128]{3,2,1,0:T(8,128)(2,1)S(1)}, bf16[1,2,512,128]{3,2,1,0:T(8,128)(2,1)S(1)}, f32[1,2,512,128]{3,2,1,0:T(8,128)S(1)}) custom-call(s32[1]{0:T(128)} %bitcast.absent_ref.refs_0_, ...), custom_call_target="tpu_custom_call", output_to_operand_aliasing={{0}: (9, {}), {1}: (10, {})} | custom-call | flops 2013265920 | bytes 2097152 | tf_op jit(solution)/shard_map/attention/pallas_call | solution.py:185
  42.7 1.3 %collective-permute-start.9 = (bf16[1,2,512,128]{3,2,1,0:T(8,128)(2,1)S(1)}, bf16[1,2,512,128]{3,2,1,0:T(8,128)(2,1)S(1)}, u32[]{:S(2)}, u32[]{:S(2)}) collective-permute-start(bf16[1,2,512,128]{3,2,1,0:T(8,128)(2,1)S(1)} %fusion.8), channel_id=1, source_target_pairs={{2,0},{3,1},{4,2},{5,3},{6,4},{7,5},{8,6},{9,7},{10,8},{11,9},{12,... | collective-permute-start | bytes 786440 | tf_op jit(solution)/shard_map/ppermute | solution.py:266
  44.0 1.2 %collective-permute-start.12 = (bf16[1,2,512,128]{3,2,1,0:T(8,128)(2,1)S(1)}, bf16[1,2,512,128]{3,2,1,0:T(8,128)(2,1)S(1)}, u32[]{:S(2)}, u32[]{:S(2)}) collective-permute-start(bf16[1,2,512,128]{3,2,1,0:T(8,128)(2,1)S(1)} %get-tuple-element.67), channel_id=1, source_target_pairs={{0,1},{1,0},{2,3},{3,2},{4,5},{5,4},{6,7},{7,6},{8,9},{9,8},{10,11... | collective-permute-start | bytes 786440 | tf_op jit(solution)/shard_map/ppermute | solution.py:260
  45.1 2.2 %collective-permute-done.8.refs_5_.refs_6_ = bf16[1,2,512,128]{3,2,1,0:T(8,128)(2,1)S(1)} collective-permute-done((bf16[1,2,512,128]{3,2,1,0:T(8,128)(2,1)S(1)}, bf16[1,2,512,128]{3,2,1,0:T(8,128)(2,1)S(1)}, u32[]{:S(2)}, u32[]{:S(2)}) %collective-permute-start.8) | collective-permute-done | bytes 262176 | tf_op jit(solution)/shard_map/ppermute | solution.py:257
  47.3 5.2 %attention.7 = (bf16[512,1024]{1,0:T(8,128)(2,1)}, bf16[512,1024]{1,0:T(8,128)(2,1)}, bf16[1,2,512,128]{3,2,1,0:T(8,128)(2,1)S(1)}, bf16[1,2,512,128]{3,2,1,0:T(8,128)(2,1)S(1)}, f32[1,2,512,128]{3,2,1,0:T(8,128)S(1)}) custom-call(s32[1]{0:T(128)} %bitcast.absent_ref.refs_0_, ...), custom_call_target="tpu_custom_call", output_to_operand_aliasing={{0}: (9, {}), {1}: (10, {})} | custom-call | flops 2013265920 | bytes 2097152 | tf_op jit(solution)/shard_map/attention/pallas_call | solution.py:185
  53.0 2.8 %collective-permute-start.11 = (bf16[1,2,512,128]{3,2,1,0:T(8,128)(2,1)S(1)}, bf16[1,2,512,128]{3,2,1,0:T(8,128)(2,1)S(1)}, u32[]{:S(2)}, u32[]{:S(2)}) collective-permute-start(bf16[1,2,512,128]{3,2,1,0:T(8,128)(2,1)S(1)} %fusion.9), channel_id=1, source_target_pairs={{2,0},{3,1},{4,2},{5,3},{6,4},{7,5},{8,6},{9,7},{10,8},{11,9},{12,... | collective-permute-start | bytes 786440 | tf_op jit(solution)/shard_map/ppermute | solution.py:266
  55.8 2.7 %collective-permute-done.12 = bf16[1,2,512,128]{3,2,1,0:T(8,128)(2,1)S(1)} collective-permute-done((bf16[1,2,512,128]{3,2,1,0:T(8,128)(2,1)S(1)}, bf16[1,2,512,128]{3,2,1,0:T(8,128)(2,1)S(1)}, u32[]{:S(2)}, u32[]{:S(2)}) %collective-permute-start.12) | collective-permute-done | bytes 262176 | tf_op jit(solution)/shard_map/ppermute | solution.py:260
  58.6 1.3 %collective-permute-start.13 = (bf16[1,2,512,128]{3,2,1,0:T(8,128)(2,1)S(1)}, bf16[1,2,512,128]{3,2,1,0:T(8,128)(2,1)S(1)}, u32[]{:S(2)}, u32[]{:S(2)}) collective-permute-start(bf16[1,2,512,128]{3,2,1,0:T(8,128)(2,1)S(1)} %fusion.10), channel_id=1, source_target_pairs={{2,0},{3,1},{4,2},{5,3},{6,4},{7,5},{8,6},{9,7},{10,8},{11,9},{12,... | collective-permute-start | bytes 786440 | tf_op jit(solution)/shard_map/ppermute | solution.py:266
  60.0 4.2 %collective-permute-done.14 = bf16[1,2,512,128]{3,2,1,0:T(8,128)(2,1)S(1)} collective-permute-done((bf16[1,2,512,128]{3,2,1,0:T(8,128)(2,1)S(1)}, bf16[1,2,512,128]{3,2,1,0:T(8,128)(2,1)S(1)}, u32[]{:S(2)}, u32[]{:S(2)}) %collective-permute-start.14) | collective-permute-done | bytes 262176 | tf_op jit(solution)/shard_map/ppermute | solution.py:260
  64.7 3.2 %collective-permute-done.13 = bf16[1,2,512,128]{3,2,1,0:T(8,128)(2,1)S(1)} collective-permute-done((bf16[1,2,512,128]{3,2,1,0:T(8,128)(2,1)S(1)}, bf16[1,2,512,128]{3,2,1,0:T(8,128)(2,1)S(1)}, u32[]{:S(2)}, u32[]{:S(2)}) %collective-permute-start.13) | collective-permute-done | bytes 262176 | tf_op jit(solution)/shard_map/ppermute | solution.py:266
  68.1 5.6 %collective-permute-done.15 = bf16[1,2,512,128]{3,2,1,0:T(8,128)(2,1)S(1)} collective-permute-done((bf16[1,2,512,128]{3,2,1,0:T(8,128)(2,1)S(1)}, bf16[1,2,512,128]{3,2,1,0:T(8,128)(2,1)S(1)}, u32[]{:S(2)}, u32[]{:S(2)}) %collective-permute-start.15) | collective-permute-done | bytes 262176 | tf_op jit(solution)/shard_map/ppermute | solution.py:266
  73.9 1.1 %pad_maximum_fusion = (bf16[512,512]{1,0:T(8,128)(2,1)}, bf16[512,512]{1,0:T(8,128)(2,1)}) fusion(bf16[512,128]{1,0:T(8,128)(2,1)S(1)} %get-tuple-element.87, bf16[512,128]{1,0:T(8,128)(2,1)S(1)} %get-tuple-element.85, bf16[512,128]{1,0:T(8,128)(2,1)S(1)} %get-tuple-element.83, bf16[512,128]{1,0:T(8,128)(2,1)S(1)} %get-tuple-element.81, ...), kind=kLoop, calls=%fused_computation.20 | loop fusion | flops 4194304 | bytes 2097152 | tf_op jit(solution)/shard_map/concatenate | solution.py:311
  (49 shorter events, 8.2 us)
Async XLA Ops:
  0.6 1.3 %copy-start = (bf16[512,512]{1,0:T(8,128)(2,1)S(1)}, bf16[512,512]{1,0:T(8,128)(2,1)}, u32[]{:S(2)}) copy-start(bf16[512,512]{1,0:T(8,128)(2,1)} %refs_8_.5) | copy-start | bytes 1572868
  2.0 3.1 %copy-start.5 = (bf16[512,128]{1,0:T(8,128)(2,1)}, bf16[512,128]{1,0:T(8,128)(2,1)S(1)}, u32[]{:S(2)}) copy-start(bf16[512,128]{1,0:T(8,128)(2,1)S(1)} %get-tuple-element.79) | copy-start | bytes 393220
  2.1 9.7 %collective-permute-start.1 = (bf16[1,2,512,128]{3,2,1,0:T(8,128)(2,1)S(1)}, bf16[1,2,512,128]{3,2,1,0:T(8,128)(2,1)S(1)}, u32[]{:S(2)}, u32[]{:S(2)}) collective-permute-start(bf16[1,2,512,128]{3,2,1,0:T(8,128)(2,1)S(1)} %maximum_bitcast_fusion.1), channel_id=1, source_target_pairs={{0,2},{1,3},{2,4},{3,5},{4,6},{5,7},{6,8},{7,9},{8,10},{9,11},{10,... | collective-permute-start | bytes 786440 | tf_op jit(solution)/shard_map/ppermute | solution.py:253
  5.8 11.4 %collective-permute-start = (bf16[1,2,512,128]{3,2,1,0:T(8,128)(2,1)}, bf16[1,2,512,128]{3,2,1,0:T(8,128)(2,1)S(1)}, u32[]{:S(2)}, u32[]{:S(2)}) collective-permute-start(bf16[1,2,512,128]{3,2,1,0:T(8,128)(2,1)} %maximum_bitcast_fusion), channel_id=1, source_target_pairs={{0,2},{1,3},{2,4},{3,5},{4,6},{5,7},{6,8},{7,9},{8,10},{9,11},{10,... | collective-permute-start | bytes 786440 | tf_op jit(solution)/shard_map/ppermute | solution.py:253
  7.1 14.2 %copy-start.2 = (bf16[512,1024]{1,0:T(8,128)(2,1)S(1)}, bf16[512,1024]{1,0:T(8,128)(2,1)}, u32[]{:S(2)}) copy-start(bf16[512,1024]{1,0:T(8,128)(2,1)} %refs_1_.5) | copy-start | bytes 3145732
  12.6 8.7 %collective-permute-start.2 = (bf16[1,2,512,128]{3,2,1,0:T(8,128)(2,1)}, bf16[1,2,512,128]{3,2,1,0:T(8,128)(2,1)S(1)}, u32[]{:S(2)}, u32[]{:S(2)}) collective-permute-start(bf16[1,2,512,128]{3,2,1,0:T(8,128)(2,1)} %broadcast_select_fusion.2), channel_id=1, source_target_pairs={{0,1},{1,0},{2,3},{3,2},{4,5},{5,4},{6,7},{7,6},{8,9},{9,8},{10,11... | collective-permute-start | bytes 786440 | tf_op jit(solution)/shard_map/ppermute | solution.py:257
  15.1 6.1 %copy-start.1 = (bf16[512,512]{1,0:T(8,128)(2,1)S(1)}, bf16[512,512]{1,0:T(8,128)(2,1)}, u32[]{:S(2)}) copy-start(bf16[512,512]{1,0:T(8,128)(2,1)} %refs_7_.5) | copy-start | bytes 1572868
  15.1 4.0 %copy-start.6 = (bf16[1,2,512,128]{3,2,1,0:T(8,128)(2,1)S(1)}, bf16[1,2,512,128]{3,2,1,0:T(8,128)(2,1)}, u32[]{:S(2)}) copy-start(bf16[1,2,512,128]{3,2,1,0:T(8,128)(2,1)} %maximum_bitcast_fusion.2) | copy-start | bytes 786436
  15.1 12.6 %collective-permute-start.5 = (bf16[1,2,512,128]{3,2,1,0:T(8,128)(2,1)}, bf16[1,2,512,128]{3,2,1,0:T(8,128)(2,1)S(1)}, u32[]{:S(2)}, u32[]{:S(2)}) collective-permute-start(bf16[1,2,512,128]{3,2,1,0:T(8,128)(2,1)} %maximum_bitcast_fusion.3), channel_id=1, source_target_pairs={{0,2},{1,3},{2,4},{3,5},{4,6},{5,7},{6,8},{7,9},{8,10},{9,11},{10,... | collective-permute-start | bytes 786440 | tf_op jit(solution)/shard_map/ppermute | solution.py:253
  18.2 11.7 %collective-permute-start.6 = (bf16[1,2,512,128]{3,2,1,0:T(8,128)(2,1)S(1)}, bf16[1,2,512,128]{3,2,1,0:T(8,128)(2,1)S(1)}, u32[]{:S(2)}, u32[]{:S(2)}) collective-permute-start(bf16[1,2,512,128]{3,2,1,0:T(8,128)(2,1)S(1)} %broadcast_select_fusion.3), channel_id=1, source_target_pairs={{0,1},{1,0},{2,3},{3,2},{4,5},{5,4},{6,7},{7,6},{8,9},{9,8},{10,11... | collective-permute-start | bytes 786440 | tf_op jit(solution)/shard_map/ppermute | solution.py:257
  19.2 15.9 %collective-permute-start.4 = (bf16[1,2,512,128]{3,2,1,0:T(8,128)(2,1)S(1)}, bf16[1,2,512,128]{3,2,1,0:T(8,128)(2,1)S(1)}, u32[]{:S(2)}, u32[]{:S(2)}) collective-permute-start(bf16[1,2,512,128]{3,2,1,0:T(8,128)(2,1)S(1)} %copy-done.6), channel_id=1, source_target_pairs={{0,2},{1,3},{2,4},{3,5},{4,6},{5,7},{6,8},{7,9},{8,10},{9,11},{10,... | collective-permute-start | bytes 786440 | tf_op jit(solution)/shard_map/ppermute | solution.py:253
  21.3 1.2 %copy-start.3 = (bf16[512,1024]{1,0:T(8,128)(2,1)S(1)}, bf16[512,1024]{1,0:T(8,128)(2,1)}, u32[]{:S(2)}) copy-start(bf16[512,1024]{1,0:T(8,128)(2,1)} %refs_2_.5) | copy-start | bytes 3145732
  22.5 7.4 %copy-start.4 = (bf16[512,1024]{1,0:T(8,128)(2,1)S(1)}, bf16[512,1024]{1,0:T(8,128)(2,1)}, u32[]{:S(2)}) copy-start(bf16[512,1024]{1,0:T(8,128)(2,1)} %refs_2_.5) | copy-start | bytes 3145732
  27.8 8.5 %collective-permute-start.7 = (bf16[1,2,512,128]{3,2,1,0:T(8,128)(2,1)S(1)}, bf16[1,2,512,128]{3,2,1,0:T(8,128)(2,1)S(1)}, u32[]{:S(2)}, u32[]{:S(2)}) collective-permute-start(bf16[1,2,512,128]{3,2,1,0:T(8,128)(2,1)S(1)} %broadcast_select_fusion.1), channel_id=1, source_target_pairs={{0,1},{1,0},{2,3},{3,2},{4,5},{5,4},{6,7},{7,6},{8,9},{9,8},{10,11... | collective-permute-start | bytes 786440 | tf_op jit(solution)/shard_map/ppermute | solution.py:257
  28.9 12.8 %collective-permute-start.3 = (bf16[1,2,512,128]{3,2,1,0:T(8,128)(2,1)S(1)}, bf16[1,2,512,128]{3,2,1,0:T(8,128)(2,1)S(1)}, u32[]{:S(2)}, u32[]{:S(2)}) collective-permute-start(bf16[1,2,512,128]{3,2,1,0:T(8,128)(2,1)S(1)} %get-tuple-element.40), channel_id=1, source_target_pairs={{0,1},{1,0},{2,3},{3,2},{4,5},{5,4},{6,7},{7,6},{8,9},{9,8},{10,11... | collective-permute-start | bytes 786440 | tf_op jit(solution)/shard_map/ppermute | solution.py:260
  35.1 12.2 %collective-permute-start.8 = (bf16[1,2,512,128]{3,2,1,0:T(8,128)(2,1)S(1)}, bf16[1,2,512,128]{3,2,1,0:T(8,128)(2,1)S(1)}, u32[]{:S(2)}, u32[]{:S(2)}) collective-permute-start(bf16[1,2,512,128]{3,2,1,0:T(8,128)(2,1)S(1)} %broadcast_select_fusion), channel_id=1, source_target_pairs={{0,1},{1,0},{2,3},{3,2},{4,5},{5,4},{6,7},{7,6},{8,9},{9,8},{10,11... | collective-permute-start | bytes 786440 | tf_op jit(solution)/shard_map/ppermute | solution.py:257
  41.7 11.2 %collective-permute-start.10 = (bf16[1,2,512,128]{3,2,1,0:T(8,128)(2,1)S(1)}, bf16[1,2,512,128]{3,2,1,0:T(8,128)(2,1)S(1)}, u32[]{:S(2)}, u32[]{:S(2)}) collective-permute-start(bf16[1,2,512,128]{3,2,1,0:T(8,128)(2,1)S(1)} %get-tuple-element.62), channel_id=1, source_target_pairs={{0,1},{1,0},{2,3},{3,2},{4,5},{5,4},{6,7},{7,6},{8,9},{9,8},{10,11... | collective-permute-start | bytes 786440 | tf_op jit(solution)/shard_map/ppermute | solution.py:260
  42.7 21.5 %collective-permute-start.9 = (bf16[1,2,512,128]{3,2,1,0:T(8,128)(2,1)S(1)}, bf16[1,2,512,128]{3,2,1,0:T(8,128)(2,1)S(1)}, u32[]{:S(2)}, u32[]{:S(2)}) collective-permute-start(bf16[1,2,512,128]{3,2,1,0:T(8,128)(2,1)S(1)} %fusion.8), channel_id=1, source_target_pairs={{2,0},{3,1},{4,2},{5,3},{6,4},{7,5},{8,6},{9,7},{10,8},{11,9},{12,... | collective-permute-start | bytes 786440 | tf_op jit(solution)/shard_map/ppermute | solution.py:266
  44.0 14.6 %collective-permute-start.12 = (bf16[1,2,512,128]{3,2,1,0:T(8,128)(2,1)S(1)}, bf16[1,2,512,128]{3,2,1,0:T(8,128)(2,1)S(1)}, u32[]{:S(2)}, u32[]{:S(2)}) collective-permute-start(bf16[1,2,512,128]{3,2,1,0:T(8,128)(2,1)S(1)} %get-tuple-element.67), channel_id=1, source_target_pairs={{0,1},{1,0},{2,3},{3,2},{4,5},{5,4},{6,7},{7,6},{8,9},{9,8},{10,11... | collective-permute-start | bytes 786440 | tf_op jit(solution)/shard_map/ppermute | solution.py:260
  52.5 11.7 %collective-permute-start.14 = (bf16[1,2,512,128]{3,2,1,0:T(8,128)(2,1)S(1)}, bf16[1,2,512,128]{3,2,1,0:T(8,128)(2,1)S(1)}, u32[]{:S(2)}, u32[]{:S(2)}) collective-permute-start(bf16[1,2,512,128]{3,2,1,0:T(8,128)(2,1)S(1)} %get-tuple-element.70), channel_id=1, source_target_pairs={{0,1},{1,0},{2,3},{3,2},{4,5},{5,4},{6,7},{7,6},{8,9},{9,8},{10,11... | collective-permute-start | bytes 786440 | tf_op jit(solution)/shard_map/ppermute | solution.py:260
  53.0 14.9 %collective-permute-start.11 = (bf16[1,2,512,128]{3,2,1,0:T(8,128)(2,1)S(1)}, bf16[1,2,512,128]{3,2,1,0:T(8,128)(2,1)S(1)}, u32[]{:S(2)}, u32[]{:S(2)}) collective-permute-start(bf16[1,2,512,128]{3,2,1,0:T(8,128)(2,1)S(1)} %fusion.9), channel_id=1, source_target_pairs={{2,0},{3,1},{4,2},{5,3},{6,4},{7,5},{8,6},{9,7},{10,8},{11,9},{12,... | collective-permute-start | bytes 786440 | tf_op jit(solution)/shard_map/ppermute | solution.py:266
  58.6 9.2 %collective-permute-start.13 = (bf16[1,2,512,128]{3,2,1,0:T(8,128)(2,1)S(1)}, bf16[1,2,512,128]{3,2,1,0:T(8,128)(2,1)S(1)}, u32[]{:S(2)}, u32[]{:S(2)}) collective-permute-start(bf16[1,2,512,128]{3,2,1,0:T(8,128)(2,1)S(1)} %fusion.10), channel_id=1, source_target_pairs={{2,0},{3,1},{4,2},{5,3},{6,4},{7,5},{8,6},{9,7},{10,8},{11,9},{12,... | collective-permute-start | bytes 786440 | tf_op jit(solution)/shard_map/ppermute | solution.py:266
  64.4 9.3 %collective-permute-start.15 = (bf16[1,2,512,128]{3,2,1,0:T(8,128)(2,1)S(1)}, bf16[1,2,512,128]{3,2,1,0:T(8,128)(2,1)S(1)}, u32[]{:S(2)}, u32[]{:S(2)}) collective-permute-start(bf16[1,2,512,128]{3,2,1,0:T(8,128)(2,1)S(1)} %fusion.11), channel_id=1, source_target_pairs={{2,0},{3,1},{4,2},{5,3},{6,4},{7,5},{8,6},{9,7},{10,8},{11,9},{12,... | collective-permute-start | bytes 786440 | tf_op jit(solution)/shard_map/ppermute | solution.py:266
